TPU v7x, 32 devices: a whole 2x2x4 slice. The times are simulated.
32 devices in a mesh: row: 8 (over z, x), col: 4 (over y, core).
Axes of the slice: x: 2, y: 2, z: 4, core: 2. Of those that a mesh axis runs over, the one named last changes fastest.
Arguments:
- object_field: float32 [2, 2048, 4096], P(None, 'row', 'col'), may hold values from -4.2 to 4.2
- probe: float32 [2, 128, 128], replicated, may hold values from -4.2 to 4.2
- position: int32 [8, 4, 48, 2], P('row', 'col'), may hold values from 0 to 1023, as said below
- live_count: int32 [8, 4], P('row', 'col'), may hold values from 1 to 48, as said below
- intensity: float32 [8, 4, 48, 128, 128], P('row', 'col'), may hold values from 0 to 3
Outputs:
- object_out: float32 [2, 2048, 4096], P(None, 'row', 'col')
- probe_out: float32 [2, 128, 128], replicated
Inputs may be any that keep to these rules, and one draw needn't show every extreme that they name: `position`: every patch lies inside the object: tiles of the last row have first rows up to 128, tiles of the last column first columns up to 896. Slots 0 to live_count - 1 of a tile are live; in every draw some tile has all 48 slots live.
All inputs are finite; a program needn't handle non-finite values.
Results may differ from a plain program's by a relative error of at most 0.0003.
Values sent between devices are 32-bit elements; how exact they have to be, the bound alone decides.
A program may use at most 128 MiB of HBM per device.

v0:
```python
import math

import jax
import jax.numpy as jnp
from jax import lax
from jax.sharding import PartitionSpec as P

BLK = 8
ITERS = 2


FULL_PRECISION = lax.Precision.HIGHEST
STEP_OBJECT = 0.05
STEP_PROBE = 0.25


def shifted(block, axis, distance):
    devices = range(lax.axis_size(axis))
    route = [(i - distance, i) for i in devices if i - distance in devices]
    return lax.ppermute(block, axis, route)


def fourier_tables(length):
    indices = jnp.arange(length, dtype=jnp.int32)
    product = indices[:, None] * indices[None, :] % length
    angles = product.astype(jnp.float32) * (2.0 * math.pi / length)
    return (jnp.cos(angles), jnp.sin(angles))


def left_mul(table, stack_in):
    return jnp.einsum("kn,bnm->bkm", table, stack_in, precision=FULL_PRECISION)


def right_mul(stack_in, table):
    return jnp.einsum("bkn,nm->bkm", stack_in, table, precision=FULL_PRECISION)


def transform(real_in, imag_in, cos_table, sin_table, direction):
    left_re = left_mul(cos_table, real_in) - direction * left_mul(sin_table, imag_in)
    left_im = left_mul(cos_table, imag_in) + direction * left_mul(sin_table, real_in)
    out_re = right_mul(left_re, cos_table) - direction * right_mul(left_im, sin_table)
    out_im = right_mul(left_im, cos_table) + direction * right_mul(left_re, sin_table)
    scale = 1.0 / cos_table.shape[0]
    return (out_re * scale, out_im * scale)


def wave_terms(patches, probe_now, measured, live_mask, cos_table, sin_table):
    obj_re, obj_im = (patches[:, 0], patches[:, 1])
    prb_re, prb_im = (probe_now[0], probe_now[1])
    psi_re = prb_re * obj_re - prb_im * obj_im
    psi_im = prb_re * obj_im + prb_im * obj_re
    far_re, far_im = transform(psi_re, psi_im, cos_table, sin_table, -1.0)
    power = far_re * far_re + far_im * far_im
    weight = 2.0 * (power - measured) * live_mask[:, None, None]
    back_re, back_im = transform(weight * far_re, weight * far_im, cos_table, sin_table, 1.0)
    grad_re = prb_re * back_re + prb_im * back_im
    grad_im = prb_re * back_im - prb_im * back_re
    probe_re = jnp.sum(obj_re * back_re + obj_im * back_im, axis=0)
    probe_im = jnp.sum(obj_re * back_im - obj_im * back_re, axis=0)
    return (jnp.stack([grad_re, grad_im], axis=1), jnp.stack([probe_re, probe_im], axis=0))


def accumulate(extended, probe_now, coords, measured, end_slot, cos_table, sin_table):
    slot_count = coords.shape[0]
    side_len = probe_now.shape[1]
    zero_start = jnp.int32(0)
    blocks = (jnp.maximum(end_slot, 0) + BLK - 1) // BLK

    def block_step(block_index, carry):
        gradient, probe_grad = carry
        begin_slot = block_index * BLK
        anchor = jnp.minimum(begin_slot, slot_count - BLK)
        slot_ids = anchor + jnp.arange(BLK, dtype=jnp.int32)
        live_mask = ((slot_ids >= begin_slot) & (slot_ids < end_slot)).astype(jnp.float32)
        places = lax.dynamic_slice_in_dim(coords, anchor, BLK, 0)
        values = lax.dynamic_slice_in_dim(measured, anchor, BLK, 0)

        def take_patch(row_at, col_at):
            return lax.dynamic_slice(
                extended, (zero_start, row_at, col_at), (2, side_len, side_len)
            )

        patches = jax.vmap(take_patch)(places[:, 0], places[:, 1])
        grad_patch, grad_probe = wave_terms(
            patches, probe_now, values, live_mask, cos_table, sin_table
        )

        def place_one(member, total):
            row_at = places[member, 0]
            col_at = places[member, 1]
            current = lax.dynamic_slice(
                total, (zero_start, row_at, col_at), (2, side_len, side_len)
            )
            return lax.dynamic_update_slice(
                total, current + grad_patch[member], (zero_start, row_at, col_at)
            )

        gradient = lax.fori_loop(0, BLK, place_one, gradient)
        return (gradient, probe_grad + grad_probe)

    start = (jnp.zeros_like(extended), jnp.zeros_like(probe_now))
    return lax.fori_loop(jnp.int32(0), blocks, block_step, start)


def body(object_field, probe, position, live_count, intensity):
    side_len = probe.shape[1]
    rows_here = object_field.shape[1]
    cols_here = object_field.shape[2]
    coords = position[0, 0]
    measured = intensity[0, 0]
    live_here = live_count[0, 0]
    cos_table, sin_table = fourier_tables(side_len)
    object_now, probe_now = (object_field, probe)
    for sweep in range(ITERS):
        below = shifted(object_now[:, :side_len, :], "row", -1)
        tall_tile = jnp.concatenate([object_now, below], axis=1)
        beside = shifted(tall_tile[:, :, :side_len], "col", -1)
        extended = jnp.concatenate([tall_tile, beside], axis=2)
        gradient, probe_grad = accumulate(
            extended, probe_now, coords, measured, live_here, cos_table, sin_table
        )
        probe_total, live_total = lax.psum(
            (probe_grad, live_here.astype(jnp.float32)), ("row", "col")
        )
        spill = shifted(gradient[:, :, cols_here:], "col", 1)
        tall_grad = gradient[:, :, :cols_here]
        tall_grad = tall_grad.at[:, :, :side_len].add(spill)
        lower = shifted(tall_grad[:, rows_here:, :], "row", 1)
        own_grad = tall_grad[:, :rows_here, :].at[:, :side_len, :].add(lower)
        object_now = object_now - STEP_OBJECT * own_grad
        probe_now = probe_now - STEP_PROBE * probe_total / live_total
    return (object_now, probe_now)


def solution(mesh):
    placed = (
        P(None, "row", "col"),
        P(),
        P("row", "col", None, None),
        P("row", "col"),
        P("row", "col", None, None, None),
    )
    return jax.shard_map(
        body, mesh=mesh, in_specs=placed, out_specs=(P(None, "row", "col"), P()), check_vma=False
    )
```

profile of v0, /device:TPU:20, one launch (start us, length us, event | category | flops | bytes accessed | tf_op | source)
XLA Modules:
  0.0 1814.3 jit_solution(11482306841915385779)
XLA Ops:
  8.7 3.3 collective-permute-start
  12.2 23.2 %collective-permute-done = f32[2,128,1024]{2,1,0:T(8,128)S(1)} collective-permute-done((f32[2,128,1024]{2,1,0:T(8,128)S(1)}, f32[2,128,1024]{2,1,0:T(8,128)S(1)}, u32[]{:S(2)}, u32[]{:S(2)}) %collective-permute-start) | collective-permute-done | bytes 1048608 | tf_op jit(solution)/shard_map/ppermute | solution.py:20
  39.9 4.6 collective-permute-done.1
  44.5 3.9 pad_maximum_fusion.2
  50.5 234.5 %while.72 = (s32[]{:T(128)}, f32[2,384,1152]{2,1,0:T(8,128)}, f32[2,128,128]{2,1,0:T(8,128)S(1)}, s32[]{:T(128)}, s32[48,2]{0,1:T(2,128)S(1)}, /*index=5*/f32[2,...) while((s32[]{:T(128)}, f32[2,384,1152]{2,1,0:T(8,128)}, ...), condition=%wide.region_5.6_spmd.clone.clone, body=%wide.region_0.5_spmd.clone.clone.sunk | while | flops 3231678464 | bytes 31458520 | solution.py:102
  51.3 23.9 %while.76 = (s32[]{:T(128)}, f32[2,384,1152]{2,1,0:T(8,128)}, s32[8,3]{0,1:T(4,128)S(1)}, f32[8,2,128,128]{3,2,0,1:T(8,128)S(1)}, s32[]{:T(128)}) while((s32[]{:T(128)}, f32[2,384,1152]{2,1,0:T(8,128)}, s32[8,3]{0,1:T(4,128)S(1)}, f32[8,2,128,128]{3,2,0,1:T(8,128)S(1)}, s32[]{:T(128)}) %tuple.209), condition=%wide.while_cond.4, body=%wide.while_body.4.sunk | while | flops 2 | bytes 262269 | solution.py:79
  55.0 2.3 bitcast_dynamic-update-slice_fusion.5
  58.0 2.3 bitcast_dynamic-update-slice_fusion.5
  60.9 2.3 bitcast_dynamic-update-slice_fusion.5
  63.9 2.3 bitcast_dynamic-update-slice_fusion.5
  66.9 2.3 bitcast_dynamic-update-slice_fusion.5
  72.9 2.3 bitcast_dynamic-update-slice_fusion.5
  94.9 72.7 %while.77 = (s32[]{:T(128)}, f32[2,384,1152]{2,1,0:T(8,128)}, s32[8,2]{0,1:T(2,128)S(1)}, f32[8,2,128,128]{3,2,0,1:T(8,128)S(1)}, s32[]{:T(128)}, /*index=5*/s32[]{:T(128)}, s32[]{:T(128)}, s32[]{:T(128)}) while((s32[]{:T(128)}, f32[2,384,1152]{2,1,0:T(8,128)}, s32[8,2]{0,1:T(2,128)S(1)}, f32[8,2,128,128]{3,2,0,1:T(8,128)S(1)}, s32[]{:T(128)}, ...), condition=%wide.region_2.2_spmd, body=%wide.region_1.1_spmd.sunk | while | flops 32776 | bytes 655557 | solution.py:98
  100.4 3.7 dynamic_update_slice.17
  109.5 3.7 dynamic_update_slice.17
  118.6 3.7 dynamic_update_slice.17
  127.8 3.7 dynamic_update_slice.17
  136.9 3.7 dynamic_update_slice.17
  146.0 3.5 dynamic_update_slice.17
  155.0 3.7 dynamic_update_slice.17
  164.2 3.4 dynamic_update_slice.17
  168.4 23.9 %while.76 = (s32[]{:T(128)}, f32[2,384,1152]{2,1,0:T(8,128)}, s32[8,3]{0,1:T(4,128)S(1)}, f32[8,2,128,128]{3,2,0,1:T(8,128)S(1)}, s32[]{:T(128)}) while((s32[]{:T(128)}, f32[2,384,1152]{2,1,0:T(8,128)}, s32[8,3]{0,1:T(4,128)S(1)}, f32[8,2,128,128]{3,2,0,1:T(8,128)S(1)}, s32[]{:T(128)}) %tuple.209), condition=%wide.while_cond.4, body=%wide.while_body.4.sunk | while | flops 2 | bytes 262269 | solution.py:79
  169.0 2.3 bitcast_dynamic-update-slice_fusion.5
  212.0 72.7 %while.77 = (s32[]{:T(128)}, f32[2,384,1152]{2,1,0:T(8,128)}, s32[8,2]{0,1:T(2,128)S(1)}, f32[8,2,128,128]{3,2,0,1:T(8,128)S(1)}, s32[]{:T(128)}, /*index=5*/s32[]{:T(128)}, s32[]{:T(128)}, s32[]{:T(128)}) while((s32[]{:T(128)}, f32[2,384,1152]{2,1,0:T(8,128)}, s32[8,2]{0,1:T(2,128)S(1)}, f32[8,2,128,128]{3,2,0,1:T(8,128)S(1)}, s32[]{:T(128)}, ...), condition=%wide.region_2.2_spmd, body=%wide.region_1.1_spmd.sunk | while | flops 32776 | bytes 655557 | solution.py:98
  217.4 3.7 dynamic_update_slice.17
  226.6 3.5 dynamic_update_slice.17
  235.5 3.7 dynamic_update_slice.17
  244.6 3.7 dynamic_update_slice.17
  253.8 3.7 dynamic_update_slice.17
  262.9 3.4 dynamic_update_slice.17
  271.8 3.7 dynamic_update_slice.17
  281.0 3.7 dynamic_update_slice.17
  286.1 467.2 %collective-permute-start.2 = (f32[2,384,128]{2,1,0:T(8,128)S(1)}, f32[2,384,128]{2,1,0:T(8,128)S(1)}, u32[]{:S(2)}, u32[]{:S(2)}) collective-permute-start(f32[2,384,128]{2,1,0:T(8,128)S(1)} %slice.176), channel_id=1, source_target_pairs={{0,1},{1,2},{2,3},{4,5},{5,6},{6,7},{8,9},{9,10},{10,11},{12,13},{... | collective-permute-start | bytes 1179656 | tf_op jit(solution)/shard_map/ppermute | solution.py:20
  756.6 12.8 collective-permute-start.3
  769.7 28.1 %collective-permute-done.3 = f32[2,128,1024]{2,1,0:T(8,128)S(1)} collective-permute-done((f32[2,128,1024]{2,1,0:T(8,128)S(1)}, f32[2,128,1024]{2,1,0:T(8,128)S(1)}, u32[]{:S(2)}, u32[]{:S(2)}) %collective-permute-start.3) | collective-permute-done | bytes 1048608 | tf_op jit(solution)/shard_map/ppermute | solution.py:20
  800.4 15.2 collective-permute-done.4
  816.4 3.0 collective-permute-start.5
  819.5 42.7 %psum.25 = f32[]{:T(128)} all-reduce(f32[]{:T(128)S(6)} %convert_element_type.80), channel_id=1, replica_groups=mesh['row'=8,'col'=4] {'row','col'}, use_global_device_ids=true, to_apply=%region_7.8 | all-reduce | flops 1 | bytes 8 | tf_op jit(solution)/shard_map/psum | solution.py:122
  862.2 80.1 %all-reduce.3.cloned.1.call-done = f32[2,128,128]{2,1,0:T(8,128)} async-done(((f32[2,128,128]{2,1,0:T(8,128)}), f32[2,128,128]{2,1,0:T(8,128)}) %all-reduce.3.cloned.1.call-update) | async-done | bytes 131088 | tf_op jit(solution)/shard_map/psum | solution.py:122
  943.9 3.1 pad_maximum_fusion.3
  949.7 236.5 %while.75 = (s32[]{:T(128)}, f32[2,384,1152]{2,1,0:T(8,128)}, f32[2,128,128]{2,1,0:T(8,128)}, s32[]{:T(128)}, s32[48,2]{0,1:T(2,128)S(1)}, /*index=5*/f32[2,128,...) while((s32[]{:T(128)}, f32[2,384,1152]{2,1,0:T(8,128)}, ...), condition=%wide.region_13.14_spmd.clone.clone, body=%wide.region_8.13_spmd.clone.clone.sunk | while | flops 3231678464 | bytes 32507152 | solution.py:102
  950.7 22.9 %while.78 = (s32[]{:T(128)}, f32[2,384,1152]{2,1,0:T(8,128)}, s32[8,3]{0,1:T(4,128)S(1)}, f32[8,2,128,128]{3,2,0,1:T(8,128)S(1)}, s32[]{:T(128)}) while((s32[]{:T(128)}, f32[2,384,1152]{2,1,0:T(8,128)}, s32[8,3]{0,1:T(4,128)S(1)}, f32[8,2,128,128]{3,2,0,1:T(8,128)S(1)}, s32[]{:T(128)}) %tuple.203), condition=%wide.while_cond.5, body=%wide.while_body.5.sunk | while | flops 2 | bytes 262269 | solution.py:79
  994.0 73.9 %while.79 = (s32[]{:T(128)}, f32[2,384,1152]{2,1,0:T(8,128)}, s32[8,2]{0,1:T(2,128)S(1)}, f32[8,2,128,128]{3,2,0,1:T(8,128)S(1)}, s32[]{:T(128)}, /*index=5*/s32[]{:T(128)}, s32[]{:T(128)}, s32[]{:T(128)}) while((s32[]{:T(128)}, f32[2,384,1152]{2,1,0:T(8,128)}, s32[8,2]{0,1:T(2,128)S(1)}, f32[8,2,128,128]{3,2,0,1:T(8,128)S(1)}, s32[]{:T(128)}, ...), condition=%wide.region_10.10_spmd, body=%wide.region_9.9_spmd.sunk | while | flops 32776 | bytes 655557 | solution.py:98
  999.6 3.7 dynamic_update_slice.16
  1008.9 3.7 dynamic_update_slice.16
  1018.2 3.7 dynamic_update_slice.16
  1027.5 3.7 dynamic_update_slice.16
  1036.8 3.7 dynamic_update_slice.16
  1046.1 3.5 dynamic_update_slice.16
  1055.2 3.7 dynamic_update_slice.16
  1064.5 3.4 dynamic_update_slice.16
  1068.7 22.9 %while.78 = (s32[]{:T(128)}, f32[2,384,1152]{2,1,0:T(8,128)}, s32[8,3]{0,1:T(4,128)S(1)}, f32[8,2,128,128]{3,2,0,1:T(8,128)S(1)}, s32[]{:T(128)}) while((s32[]{:T(128)}, f32[2,384,1152]{2,1,0:T(8,128)}, s32[8,3]{0,1:T(4,128)S(1)}, f32[8,2,128,128]{3,2,0,1:T(8,128)S(1)}, s32[]{:T(128)}) %tuple.203), condition=%wide.while_cond.5, body=%wide.while_body.5.sunk | while | flops 2 | bytes 262269 | solution.py:79
  1112.1 73.9 %while.79 = (s32[]{:T(128)}, f32[2,384,1152]{2,1,0:T(8,128)}, s32[8,2]{0,1:T(2,128)S(1)}, f32[8,2,128,128]{3,2,0,1:T(8,128)S(1)}, s32[]{:T(128)}, /*index=5*/s32[]{:T(128)}, s32[]{:T(128)}, s32[]{:T(128)}) while((s32[]{:T(128)}, f32[2,384,1152]{2,1,0:T(8,128)}, s32[8,2]{0,1:T(2,128)S(1)}, f32[8,2,128,128]{3,2,0,1:T(8,128)S(1)}, s32[]{:T(128)}, ...), condition=%wide.region_10.10_spmd, body=%wide.region_9.9_spmd.sunk | while | flops 32776 | bytes 655557 | solution.py:98
  1117.7 3.7 dynamic_update_slice.16
  1127.0 3.5 dynamic_update_slice.16
  1136.1 3.7 dynamic_update_slice.16
  1145.3 3.7 dynamic_update_slice.16
  1154.6 3.7 dynamic_update_slice.16
  1163.9 3.4 dynamic_update_slice.16
  1173.0 3.7 dynamic_update_slice.16
  1182.3 3.7 dynamic_update_slice.16
  1187.2 473.1 %collective-permute-start.6 = (f32[2,384,128]{2,1,0:T(8,128)S(1)}, f32[2,384,128]{2,1,0:T(8,128)S(1)}, u32[]{:S(2)}, u32[]{:S(2)}) collective-permute-start(f32[2,384,128]{2,1,0:T(8,128)S(1)} %slice.184), channel_id=1, source_target_pairs={{0,1},{1,2},{2,3},{4,5},{5,6},{6,7},{8,9},{9,10},{10,11},{12,13},{... | collective-permute-start | bytes 1179656 | tf_op jit(solution)/shard_map/ppermute | solution.py:20
  1666.2 9.7 collective-permute-start.7
  1676.0 124.0 %all-reduce.5.cloned.1.call-done = f32[2,128,128]{2,1,0:T(8,128)} async-done(((f32[2,128,128]{2,1,0:T(8,128)}), f32[2,128,128]{2,1,0:T(8,128)}) %all-reduce.5.cloned.1.call-update) | async-done | bytes 131088 | tf_op jit(solution)/shard_map/psum | solution.py:122
  (315 shorter events, 248.8 us)
Async XLA Ops:
  7.2 4.8 copy-start.2
  7.2 935.2 %all-reduce.3.cloned.1.call-start = ((), (), s32[]{:S(2)}) async-start(), calls=%async_computation | async-start | bytes 262144 | tf_op jit(solution)/shard_map/psum | solution.py:122
  8.7 26.8 %collective-permute-start = (f32[2,128,1024]{2,1,0:T(8,128)S(1)}, f32[2,128,1024]{2,1,0:T(8,128)S(1)}, u32[]{:S(2)}, u32[]{:S(2)}) collective-permute-start(f32[2,128,1024]{2,1,0:T(8,128)S(1)} %slice.172), channel_id=1, source_target_pairs={{4,0},{8,4},{12,8},{16,12},{20,16},{24,20},{28,24},{5,1},{9,5},{13... | collective-permute-start | bytes 3145736 | tf_op jit(solution)/shard_map/ppermute | solution.py:20
  35.6 1.7 copy-start.4
  37.3 7.2 collective-permute-start.1
  48.5 2.0 copy-start.1
  48.5 2.0 copy-start.8
  285.0 470.4 %copy-start.7 = (f32[2,128,128]{2,1,0:T(8,128)}, f32[2,128,128]{2,1,0:T(8,128)S(1)}, u32[]{:S(2)}) copy-start(f32[2,128,128]{2,1,0:T(8,128)S(1)} %get-tuple-element.411) | copy-start | bytes 393220
  286.1 469.3 %collective-permute-start.2 = (f32[2,384,128]{2,1,0:T(8,128)S(1)}, f32[2,384,128]{2,1,0:T(8,128)S(1)}, u32[]{:S(2)}, u32[]{:S(2)}) collective-permute-start(f32[2,384,128]{2,1,0:T(8,128)S(1)} %slice.176), channel_id=1, source_target_pairs={{0,1},{1,2},{2,3},{4,5},{5,6},{6,7},{8,9},{9,10},{10,11},{12,13},{... | collective-permute-start | bytes 1179656 | tf_op jit(solution)/shard_map/ppermute | solution.py:20
  756.6 41.4 %copy-start.3 = (f32[2,256,1024]{2,1,0:T(8,128)S(1)}, f32[2,256,1024]{2,1,0:T(8,128)}, u32[]{:S(2)}) copy-start(f32[2,256,1024]{2,1,0:T(8,128)} %param.21) | copy-start | bytes 6291460
  756.6 41.2 %collective-permute-start.3 = (f32[2,128,1024]{2,1,0:T(8,128)S(1)}, f32[2,128,1024]{2,1,0:T(8,128)S(1)}, u32[]{:S(2)}, u32[]{:S(2)}) collective-permute-start(f32[2,128,1024]{2,1,0:T(8,128)S(1)} %slice.245), channel_id=1, source_target_pairs={{0,4},{4,8},{8,12},{12,16},{16,20},{20,24},{24,28},{1,5},{5,9},{9,... | collective-permute-start | bytes 3145736 | tf_op jit(solution)/shard_map/ppermute | solution.py:20
  798.5 17.1 collective-permute-start.4
  816.4 127.5 %collective-permute-start.5 = (f32[2,384,128]{2,1,0:T(8,128)}, f32[2,384,128]{2,1,0:T(8,128)}, u32[]{:S(2)}, u32[]{:S(2)}) collective-permute-start(f32[2,384,128]{2,1,0:T(8,128)} %pad_maximum_fusion.4), channel_id=1, source_target_pairs={{1,0},{2,1},{3,2},{5,4},{6,5},{7,6},{9,8},{10,9},{11,10},{13,12},{... | collective-permute-start | bytes 1179656 | tf_op jit(solution)/shard_map/ppermute | solution.py:20
  819.5 980.5 %all-reduce.5.cloned.1.call-start = ((), (), s32[]{:S(2)}) async-start(), calls=%async_computation.1 | async-start | bytes 262144 | tf_op jit(solution)/shard_map/psum | solution.py:122
  992.0 1.4 copy-start.5
  993.4 0.7 copy-start.6
  1110.0 1.4 copy-start.5
  1111.4 0.7 copy-start.6
  1187.2 475.3 %collective-permute-start.6 = (f32[2,384,128]{2,1,0:T(8,128)S(1)}, f32[2,384,128]{2,1,0:T(8,128)S(1)}, u32[]{:S(2)}, u32[]{:S(2)}) collective-permute-start(f32[2,384,128]{2,1,0:T(8,128)S(1)} %slice.184), channel_id=1, source_target_pairs={{0,1},{1,2},{2,3},{4,5},{5,6},{6,7},{8,9},{9,10},{10,11},{12,13},{... | collective-permute-start | bytes 1179656 | tf_op jit(solution)/shard_map/ppermute | solution.py:20
  1663.6 1.6 copy-start
  1666.2 137.8 %collective-permute-start.7 = (f32[2,128,1024]{2,1,0:T(8,128)}, f32[2,128,1024]{2,1,0:T(8,128)S(1)}, u32[]{:S(2)}, u32[]{:S(2)}) collective-permute-start(f32[2,128,1024]{2,1,0:T(8,128)} %slice.249), channel_id=1, source_target_pairs={{0,4},{4,8},{8,12},{12,16},{16,20},{20,24},{24,28},{1,5},{5,9},{9,... | collective-permute-start | bytes 3145736 | tf_op jit(solution)/shard_map/ppermute | solution.py:20
Sparse Core Ops, SparseCore 0:
  819.6 122.6 all-reduce.2
  1676.1 123.8 all-reduce.4
where the time goes:
time: 1840 us; the launch traced here: 1810 us
  starting transfers between devices  973 us (53%)
  waiting for transfers between devices  275 us (15%)
  local copies, waits for them, and re-layouts  251 us (14%)
  loops' own time  124 us (7%)
  matrix products  77.8 us (4%)
  other arithmetic  55.3 us (3%)
  blocking collectives  42.7 us (2%)
    ppermute x8, starting transfers between devices, shifted(): return lax.ppermute(block, axis, route)  973 us
    psum x2, waiting for transfers between devices, body(): lax.psum((probe_grad, live_here.astype(jnp.float32)), ('row', 'col'))  204 us
    another operation x4, loops' own time, block_step(): gradient = lax.fori_loop(0, BLK, place_one, gradient)  122 us
    dynamic_update_slice x32, local copies, waits for them, and re-layouts, place_one(): lax.dynamic_update_slice(total, current + grad_patch[member], (zero_start...  116 us
    gather x96, local copies, waits for them, and re-layouts  93 us
    ppermute x8, waiting for transfers between devices, shifted(): return lax.ppermute(block, axis, route)  71.2 us
    psum x1, blocking collectives, body(): lax.psum((probe_grad, live_here.astype(jnp.float32)), ('row', 'col'))  42.7 us
    dot_general x32, matrix products, right_mul(): return jnp.einsum('bkn,nm->bkm', stack_in, table, precision=FULL_PRECISION)  40.9 us
  transfers between devices with their start and end apart: 10, of which 6 were waited for; matrix products, arithmetic and copies ran while one was open for 1% of the time, Pallas kernels for 0%

commit v1 on v0

v1 whole, which is shorter than its diff:
```python
import functools

import jax
import jax.numpy as jnp
import ml_dtypes
import numpy as np
from jax import lax
from jax.experimental import pallas as pl
from jax.experimental.pallas import tpu as pltpu
from jax.sharding import PartitionSpec as P

GROUP = 4
ITERS = 2
STEP_OBJECT = 0.05
STEP_PROBE = 0.25


def shifted(block, axis, distance):
    devices = range(lax.axis_size(axis))
    route = [(i - distance, i) for i in devices if i - distance in devices]
    return lax.ppermute(block, axis, route)


def fourier_tables(length):
    indices = np.arange(length)
    angles = (indices[:, None] * indices[None, :] % length) * (2.0 * np.pi / length)
    cos, sin = np.cos(angles), np.sin(angles)
    table = np.block([[cos, sin], [-sin, cos]])

    def parts(full):
        high = full.astype(ml_dtypes.bfloat16)
        low = (full - high.astype(np.float64)).astype(ml_dtypes.bfloat16)
        return high, low

    return (*parts(table), *parts(table.T / length))


def split(value):
    high = value.astype(jnp.bfloat16)
    low = (value - high.astype(jnp.float32)).astype(jnp.bfloat16)
    return high, low


def mm(a, b):
    return jnp.dot(a, b, preferred_element_type=jnp.float32)


def left(table_high, table_low, value):
    high, low = split(value)
    return mm(table_high, high) + mm(table_high, low) + mm(table_low, high)


def right(value, table_high, table_low):
    high, low = split(value)
    return mm(high, table_high) + mm(low, table_high) + mm(high, table_low)


def slots_kernel(
    live_ref, pos_ref, own, below, beside, prb, a_hi, a_lo, t_hi, t_lo, measured,
    grad, pgrad, ext, values, sems,
):
    strips, _, rows, side = own.shape
    copies = [
        pltpu.make_async_copy(own, ext.at[pl.ds(0, strips), :, pl.ds(0, rows), :], sems.at[0]),
        pltpu.make_async_copy(below, ext.at[pl.ds(0, strips), :, pl.ds(rows, side), :], sems.at[1]),
        pltpu.make_async_copy(beside, ext.at[strips], sems.at[2]),
        pltpu.make_async_copy(measured, values, sems.at[3]),
    ]
    for copy in copies:
        copy.start()
    for strip in range(strips + 1):
        grad[strip] = jnp.zeros(grad.shape[1:], jnp.float32)
    pgrad[...] = jnp.zeros_like(pgrad)
    for copy in copies:
        copy.wait()

    live = live_ref[0]
    lane = lax.broadcasted_iota(jnp.int32, (side, side), 1)

    def block(index, _):
        places = []
        objects = []
        waves = []
        for member in range(GROUP):
            slot = index * GROUP + member
            on = slot < live
            row = jnp.where(on, pos_ref[2 * slot], 0)
            col = jnp.where(on, pos_ref[2 * slot + 1], 0)
            strip = col // side
            shift = col - strip * side
            keep = lane >= shift
            back = (side - shift) % side
            window = pl.ds(row, side)

            def take(part):
                here = ext[strip, part, window, :]
                there = ext[strip + 1, part, window, :]
                return pltpu.roll(jnp.where(keep, here, there), back, 1)

            obj_re, obj_im = take(0), take(1)
            psi_re = prb[0] * obj_re - prb[1] * obj_im
            psi_im = prb[0] * obj_im + prb[1] * obj_re
            places.append((slot, on, strip, shift, window, keep))
            objects.append((obj_re, obj_im))
            waves.append(jnp.concatenate([psi_re, psi_im], axis=1))
        half = right(jnp.concatenate(waves, axis=0), t_hi[...], t_lo[...])
        half = jnp.concatenate(
            [
                jnp.concatenate(
                    [half[m * side : (m + 1) * side, :side] for m in range(GROUP)], axis=1
                ),
                jnp.concatenate(
                    [half[m * side : (m + 1) * side, side:] for m in range(GROUP)], axis=1
                ),
            ],
            axis=0,
        )
        far = left(a_hi[...], a_lo[...], half)
        far_re, far_im = far[:side], far[side:]
        power = far_re * far_re + far_im * far_im
        wanted = jnp.concatenate([values[places[m][0]] for m in range(GROUP)], axis=1)
        scale = jnp.concatenate(
            [
                jnp.full((1, side), jnp.where(places[m][1], 2.0, 0.0), jnp.float32)
                for m in range(GROUP)
            ],
            axis=1,
        )
        weight = scale * (power - wanted)
        chi = jnp.concatenate([weight * far_re, weight * far_im], axis=0)
        half = left(t_hi[...], t_lo[...], chi)
        half = jnp.concatenate(
            [
                jnp.concatenate(
                    [
                        half[:side, m * side : (m + 1) * side],
                        half[side:, m * side : (m + 1) * side],
                    ],
                    axis=1,
                )
                for m in range(GROUP)
            ],
            axis=0,
        )
        near = right(half, a_hi[...], a_lo[...])
        sum_re = jnp.zeros((side, side), jnp.float32)
        sum_im = jnp.zeros((side, side), jnp.float32)
        for member in range(GROUP):
            slot, on, strip, shift, window, keep = places[member]
            obj_re, obj_im = objects[member]
            back_re = near[member * side : (member + 1) * side, :side]
            back_im = near[member * side : (member + 1) * side, side:]
            sum_re += obj_re * back_re + obj_im * back_im
            sum_im += obj_re * back_im - obj_im * back_re
            for part, value in (
                (0, prb[0] * back_re + prb[1] * back_im),
                (1, prb[0] * back_im - prb[1] * back_re),
            ):
                turned = pltpu.roll(value, shift, 1)
                grad[strip, part, window, :] += jnp.where(keep, turned, 0.0)
                grad[strip + 1, part, window, :] += jnp.where(keep, 0.0, turned)
        pgrad[0] += sum_re
        pgrad[1] += sum_im
        return 0

    lax.fori_loop(0, (live + GROUP - 1) // GROUP, block, 0)


def slots_call(live, places, own, below, beside, probe, tables, measured):
    strips, _, rows, side = own.shape
    shape = (strips + 1, 2, rows + side, side)
    smem = pl.BlockSpec(memory_space=pltpu.SMEM)
    vmem = pl.BlockSpec(memory_space=pltpu.VMEM)
    hbm = pl.BlockSpec(memory_space=pl.ANY)
    return pl.pallas_call(
        slots_kernel,
        out_shape=(
            jax.ShapeDtypeStruct(shape, jnp.float32),
            jax.ShapeDtypeStruct(probe.shape, jnp.float32),
        ),
        in_specs=[smem, smem, hbm, hbm, hbm, vmem, vmem, vmem, vmem, vmem, hbm],
        out_specs=(vmem, vmem),
        scratch_shapes=[
            pltpu.VMEM(shape, jnp.float32),
            pltpu.VMEM(measured.shape, jnp.float32),
            pltpu.SemaphoreType.DMA((4,)),
        ],
        compiler_params=pltpu.CompilerParams(vmem_limit_bytes=40 * 1024 * 1024),
    )(live, places, own, below, beside, probe, *tables, measured)


def body(object_field, probe, position, live_count, intensity):
    side = probe.shape[1]
    rows = object_field.shape[1]
    strips = object_field.shape[2] // side
    tables = [jnp.asarray(t) for t in fourier_tables(side)]
    places = position[0, 0].reshape(-1)
    measured = intensity[0, 0]
    live = live_count.reshape(1)
    live_total = lax.psum(live.astype(jnp.float32), ("row", "col"))
    now = object_field.reshape(2, rows, strips, side).transpose(2, 0, 1, 3)
    probe_now = probe
    for sweep in range(ITERS):
        below = shifted(now[:, :, :side, :], "row", -1)
        beside = shifted(jnp.concatenate([now[0], below[0]], axis=1), "col", -1)
        grad, probe_grad = slots_call(
            live, places, now, below, beside, probe_now, tables, measured
        )
        probe_total = lax.psum(probe_grad, ("row", "col"))
        spill = shifted(grad[strips], "col", 1)
        tall = grad[:strips].at[0].add(spill)
        lower = shifted(tall[:, :, rows:, :], "row", 1)
        own_grad = tall[:, :, :rows, :].at[:, :, :side, :].add(lower)
        now = now - STEP_OBJECT * own_grad
        probe_now = probe_now - STEP_PROBE * probe_total / live_total
    return (now.transpose(1, 2, 0, 3).reshape(object_field.shape), probe_now)


def solution(mesh):
    placed = (
        P(None, "row", "col"),
        P(),
        P("row", "col", None, None),
        P("row", "col"),
        P("row", "col", None, None, None),
    )
    return jax.shard_map(
        body, mesh=mesh, in_specs=placed, out_specs=(P(None, "row", "col"), P()), check_vma=False
    )
```

time: 1840 us -> 447 us (0.24); the launches traced: 1810 us -> 444 us
  starting transfers between devices: 973 us -> 45.7 us
  local copies, waits for them, and re-layouts: 251 us -> 22.3 us
  loops' own time: 124 us -> 0 us
  matrix products: 77.8 us -> 0 us
  other arithmetic: 55.3 us -> 8.72 us
  waiting for transfers between devices: 275 us -> 298 us
    ppermute x8, starting transfers between devices: 973 us -> 45.6 us  [shifted(): return lax.ppermute(block, axis, route)]
    another operation x10 -> x0, loops' own time: 124 us -> none  [the longest x4 122 us: block_step(): gradient = lax.fori_loop(0, BLK, place_one, gradient)]
    dynamic_update_slice x32 -> x0, local copies, waits for them, and re-layouts: 116 us -> none  [place_one(): lax.dynamic_update_slice(total, current + grad_patch[member], (zero_start...]
    gather x96 -> x0, local copies, waits for them, and re-layouts: 93 us -> none
    dot_general x64 -> x0, matrix products: 77.8 us -> none  [the longest x32 40.9 us: right_mul(): return jnp.einsum('bkn,nm->bkm', stack_in, table, precision=FULL_PRECISION)]
    add x36 -> x0, other arithmetic: 34.7 us -> none  [the longest x32 34.6 us: place_one(): current + grad_patch[member]]
    dynamic_slice x36 -> x0, local copies, waits for them, and re-layouts: 21.1 us -> none  [the longest x32 20.8 us: place_one(): col_at = places[member, 1]]
  transfers between devices with their start and end apart: 10 -> 10, of which waited for: 6 -> 8; matrix products, arithmetic and copies ran while one was open for 1% -> 2% of each run, Pallas kernels for 0% -> 0%
where the time goes in v1:
time: 447 us; the launch traced here: 444 us
  waiting for transfers between devices  298 us (67%)
  starting transfers between devices  45.7 us (10%)
  blocking collectives  42.6 us (10%)
  local copies, waits for them, and re-layouts  22.3 us (5%)
  between operations  15 us (3%)
  Pallas kernels  11.6 us (3%)
  other arithmetic  8.72 us (2%)
    psum x2, waiting for transfers between devices, body(): probe_total = lax.psum(probe_grad, ('row', 'col'))  218 us
    ppermute x8, waiting for transfers between devices, shifted(): return lax.ppermute(block, axis, route)  79.6 us
    ppermute x8, starting transfers between devices, shifted(): return lax.ppermute(block, axis, route)  45.6 us
    psum x1, blocking collectives, body(): live_total = lax.psum(live.astype(jnp.float32), ('row', 'col'))  42.6 us
    unnamed x31, local copies, waits for them, and re-layouts  13.7 us
    pallas_call x2, Pallas kernels, slots_call(): pl.pallas_call(slots_kernel, out_shape=(jax.ShapeDtypeStruct(shape, jnp.f...  11.6 us
  transfers between devices with their start and end apart: 10, of which 8 were waited for; matrix products, arithmetic and copies ran while one was open for 2% of the time, Pallas kernels for 0%

profile of v1, /device:TPU:20, one launch (start us, length us, event | category | flops | bytes accessed | tf_op | source)
XLA Modules:
  0.0 443.9 jit_solution(3373289714190744199)
XLA Ops:
  7.2 0.0 all-reduce.3.cloned.1.call-start
  7.2 2.9 copy.12
  10.1 1.9 copy.13
  12.0 0.0 copy-start
  12.0 0.0 copy-start.13
  12.0 0.0 copy-start.4
  12.1 0.0 copy-start.5
  12.1 0.0 copy-start.6
  12.1 0.1 slice.176
  12.2 3.4 collective-permute-start
  15.6 23.5 %collective-permute-done.below = f32[8,2,128,128]{3,2,1,0:T(8,128)S(1)} collective-permute-done((f32[8,2,128,128]{3,2,1,0:T(8,128)S(1)}, f32[8,2,128,128]{3,2,1,0:T(8,128)S(1)}, u32[]{:S(2)}, u32[]{:S(2)}) %collective-permute-start) | collective-permute-done | bytes 1048608 | tf_op jit(solution)/shard_map/ppermute | solution.py:21
  39.1 0.8 pad_maximum_fusion
  39.9 1.9 collective-permute-start.1
  42.4 0.0 copy-done.13
  42.4 0.7 copy.14
  43.1 0.9 reshape_squeeze.3.pos_ref
  44.0 3.4 collective-permute-done.1.beside
  47.4 0.0 copy-done.4
  47.4 1.9 copy-done.2
  49.3 0.9 copy-done.8
  50.2 0.9 copy-done.10
  51.1 6.1 %shard_map.104 = (f32[9,2,384,128]{3,2,1,0:T(8,128)S(1)}, f32[2,128,128]{2,1,0:T(8,128)}) custom-call(s32[1]{0:T(128)} %bitcast.31.live_ref, s32[96]{0:T(128)S(1)} %reshape_squeeze.3.pos_ref, f32[8,2,256,128]{3,2,1,0:T(8,128)S(1)} %bitcast.36, f32[8,2,128,128]{3,2,1,0:T(8,128)S(1)} %collective-permute-done.below, ...), custom_call_target="tpu_custom_call" | custom-call | tf_op jit(solution)/shard_map/pallas_call | solution.py:175
  57.3 3.5 collective-permute-start.2
  60.7 0.2 slice.161
  61.0 5.6 %collective-permute-done.2 = f32[2,384,128]{2,1,0:T(8,128)S(1)} collective-permute-done((f32[2,384,128]{2,1,0:T(8,128)S(1)}, f32[2,384,128]{2,1,0:T(8,128)S(1)}, u32[]{:S(2)}, u32[]{:S(2)}) %collective-permute-start.2) | collective-permute-done | bytes 393248 | tf_op jit(solution)/shard_map/ppermute | solution.py:21
  66.6 0.1 slice.181
  66.7 9.8 %collective-permute-start.3 = (f32[8,2,128,128]{3,2,1,0:T(8,128)S(1)}, f32[8,2,128,128]{3,2,1,0:T(8,128)S(1)}, u32[]{:S(2)}, u32[]{:S(2)}) collective-permute-start(f32[8,2,128,128]{3,2,1,0:T(8,128)S(1)} %slice.181), channel_id=1, source_target_pairs={{0,4},{4,8},{8,12},{12,16},{16,20},{20,24},{24,28},{1,5},{5,9},{9,... | collective-permute-start | bytes 3145736 | tf_op jit(solution)/shard_map/ppermute | solution.py:21
  76.5 0.2 slice.179
  76.7 0.0 copy-start.1
  76.7 30.3 %collective-permute-done.3 = f32[8,2,128,128]{3,2,1,0:T(8,128)S(1)} collective-permute-done((f32[8,2,128,128]{3,2,1,0:T(8,128)S(1)}, f32[8,2,128,128]{3,2,1,0:T(8,128)S(1)}, u32[]{:S(2)}, u32[]{:S(2)}) %collective-permute-start.3) | collective-permute-done | bytes 1048608 | tf_op jit(solution)/shard_map/ppermute | solution.py:21
  107.0 0.1 fusion.1
  107.1 0.3 multiply_subtract_fusion.own
  107.4 0.1 slice.182
  107.5 14.8 %collective-permute-start.4 = (f32[8,2,128,128]{3,2,1,0:T(8,128)S(1)}, f32[8,2,128,128]{3,2,1,0:T(8,128)S(1)}, u32[]{:S(2)}, u32[]{:S(2)}) collective-permute-start(f32[8,2,128,128]{3,2,1,0:T(8,128)S(1)} %slice.182), channel_id=1, source_target_pairs={{4,0},{8,4},{12,8},{16,12},{20,16},{24,20},{28,24},{5,1},{9,5},{13... | collective-permute-start | bytes 3145736 | tf_op jit(solution)/shard_map/ppermute | solution.py:21
  122.3 12.3 %collective-permute-done.4.below = f32[8,2,128,128]{3,2,1,0:T(8,128)S(1)} collective-permute-done((f32[8,2,128,128]{3,2,1,0:T(8,128)S(1)}, f32[8,2,128,128]{3,2,1,0:T(8,128)S(1)}, u32[]{:S(2)}, u32[]{:S(2)}) %collective-permute-start.4) | collective-permute-done | bytes 1048608 | tf_op jit(solution)/shard_map/ppermute | solution.py:21
  134.6 0.8 pad_maximum_fusion.1
  135.3 2.1 collective-permute-start.5
  137.4 0.0 all-reduce.3.cloned.1.call-update
  137.4 0.0 all-reduce.5.cloned.1.call-start
  137.5 42.6 %psum.22 = f32[]{:T(128)} all-reduce(f32[]{:T(128)} %bitcast.10), channel_id=1, replica_groups=mesh['row'=8,'col'=4] {'row','col'}, use_global_device_ids=true, to_apply=%region_1.0 | all-reduce | flops 1 | bytes 8 | tf_op jit(solution)/shard_map/psum | solution.py:200
  180.1 80.7 %all-reduce.3.cloned.1.call-done = f32[2,128,128]{2,1,0:T(8,128)} async-done(((f32[2,128,128]{2,1,0:T(8,128)}), f32[2,128,128]{2,1,0:T(8,128)}) %all-reduce.3.cloned.1.call-update) | async-done | bytes 131088 | tf_op jit(solution)/shard_map/psum | solution.py:209
  260.8 1.6 divide_subtract_fusion.1.prb
  262.4 0.0 collective-permute-done.5.beside
  262.4 0.0 copy-start.3
  262.4 1.9 copy-done.3
  264.3 0.9 copy-done.7
  265.2 0.9 copy-done.9
  266.1 5.5 %shard_map.105 = (f32[9,2,384,128]{3,2,1,0:T(8,128)S(1)}, f32[2,128,128]{2,1,0:T(8,128)S(1)}) custom-call(s32[1]{0:T(128)} %bitcast.33.live_ref, s32[96]{0:T(128)S(1)} %reshape_squeeze.3.pos_ref, f32[8,2,256,128]{3,2,1,0:T(8,128)S(1)} %multiply_subtract_fusion.own, f32[8,2,128,128]{3,2,1,0:T(8,128)S(1)} %collective-permute-done.4.below, ...), custom_call_target="tpu_custom_call" | custom-call | tf_op jit(solution)/shard_map/pallas_call | solution.py:175
  271.6 0.0 copy-start.11
  271.7 4.2 collective-permute-start.6
  275.9 0.3 slice.170
  276.1 4.6 %collective-permute-done.6 = f32[2,384,128]{2,1,0:T(8,128)S(1)} collective-permute-done((f32[2,384,128]{2,1,0:T(8,128)S(1)}, f32[2,384,128]{2,1,0:T(8,128)S(1)}, u32[]{:S(2)}, u32[]{:S(2)}) %collective-permute-start.6) | collective-permute-done | bytes 393248 | tf_op jit(solution)/shard_map/ppermute | solution.py:21
  280.8 1.2 slice.187
  282.0 0.8 copy-done.12
  282.8 5.9 %collective-permute-start.7 = (f32[8,2,128,128]{3,2,1,0:T(8,128)}, f32[8,2,128,128]{3,2,1,0:T(8,128)S(1)}, u32[]{:S(2)}, u32[]{:S(2)}) collective-permute-start(f32[8,2,128,128]{3,2,1,0:T(8,128)} %slice.187), channel_id=1, source_target_pairs={{0,4},{4,8},{8,12},{12,16},{16,20},{20,24},{24,28},{1,5},{5,9},{9,... | collective-permute-start | bytes 3145736 | tf_op jit(solution)/shard_map/ppermute | solution.py:21
  288.7 0.0 all-reduce.5.cloned.1.call-update
  288.8 137.7 %all-reduce.5.cloned.1.call-done = f32[2,128,128]{2,1,0:T(8,128)} async-done(((f32[2,128,128]{2,1,0:T(8,128)}), f32[2,128,128]{2,1,0:T(8,128)}) %all-reduce.5.cloned.1.call-update) | async-done | bytes 131088 | tf_op jit(solution)/shard_map/psum | solution.py:209
  426.5 2.2 divide_subtract_fusion
  428.6 1.7 slice.185
  430.4 0.0 collective-permute-done.7
  430.4 1.3 fusion
  431.7 1.6 subtract_bitcast_fusion
  433.4 1.9 copy.15
  435.3 1.8 copy.16
  (19 shorter events, 0.2 us)
Async XLA Ops:
  7.2 253.7 %all-reduce.3.cloned.1.call-start = ((), (), s32[]{:S(2)}) async-start(), calls=%async_computation | async-start | bytes 262144 | tf_op jit(solution)/shard_map/psum | solution.py:209
  12.0 45.2 %copy-start = (f32[2,256,8,128]{3,1,0,2:T(8,128)}, f32[2,256,8,128]{3,1,0,2:T(8,128)S(1)}, u32[]{:S(2)}) copy-start(f32[2,256,8,128]{3,1,0,2:T(8,128)S(1)} %copy.13) | copy-start | bytes 6291460
  12.0 30.4 %copy-start.13 = (s32[1,1,48,2]{2,3,1,0:T(2,128)S(1)}, s32[1,1,48,2]{2,3,1,0:T(2,128)}, u32[]{:S(2)}) copy-start(s32[1,1,48,2]{2,3,1,0:T(2,128)} %param.19) | copy-start | bytes 1156
  12.0 35.3 %copy-start.4 = (bf16[256,256]{1,0:T(8,128)(2,1)S(1)}, bf16[256,256]{1,0:T(8,128)(2,1)}, u32[]{:S(2)}) copy-start(bf16[256,256]{1,0:T(8,128)(2,1)} %constant.107.clone.t_lo) | copy-start | bytes 393220
  12.1 35.3 %copy-start.5 = (bf16[256,256]{1,0:T(8,128)(2,1)S(1)}, bf16[256,256]{1,0:T(8,128)(2,1)}, u32[]{:S(2)}) copy-start(bf16[256,256]{1,0:T(8,128)(2,1)} %constant.106.clone.t_hi) | copy-start | bytes 393220
  12.1 35.3 %copy-start.6 = (bf16[256,256]{1,0:T(8,128)(2,1)S(1)}, bf16[256,256]{1,0:T(8,128)(2,1)}, u32[]{:S(2)}) copy-start(bf16[256,256]{1,0:T(8,128)(2,1)} %constant.105.clone.a_lo) | copy-start | bytes 393220
  12.2 26.9 %collective-permute-start = (f32[8,2,128,128]{3,2,1,0:T(8,128)S(1)}, f32[8,2,128,128]{3,2,1,0:T(8,128)S(1)}, u32[]{:S(2)}, u32[]{:S(2)}) collective-permute-start(f32[8,2,128,128]{3,2,1,0:T(8,128)S(1)} %slice.176), channel_id=1, source_target_pairs={{4,0},{8,4},{12,8},{16,12},{20,16},{24,20},{28,24},{5,1},{9,5},{13... | collective-permute-start | bytes 3145736 | tf_op jit(solution)/shard_map/ppermute | solution.py:21
  39.9 7.5 %collective-permute-start.1 = (f32[2,384,128]{2,1,0:T(8,128)}, f32[2,384,128]{2,1,0:T(8,128)}, u32[]{:S(2)}, u32[]{:S(2)}) collective-permute-start(f32[2,384,128]{2,1,0:T(8,128)} %pad_maximum_fusion), channel_id=1, source_target_pairs={{1,0},{2,1},{3,2},{5,4},{6,5},{7,6},{9,8},{10,9},{11,10},{13,12},{... | collective-permute-start | bytes 1179656 | tf_op jit(solution)/shard_map/ppermute | solution.py:21
  47.4 1.9 copy-start.2
  49.3 0.9 copy-start.8
  50.2 0.9 copy-start.10
  57.3 9.3 %collective-permute-start.2 = (f32[2,384,128]{2,1,0:T(8,128)S(1)}, f32[2,384,128]{2,1,0:T(8,128)S(1)}, u32[]{:S(2)}, u32[]{:S(2)}) collective-permute-start(f32[2,384,128]{2,1,0:T(8,128)S(1)} %slice_bitcast_fusion.1), channel_id=1, source_target_pairs={{0,1},{1,2},{2,3},{4,5},{5,6},{6,7},{8,9},{9,10},{10,11},{12,13},{... | collective-permute-start | bytes 1179656 | tf_op jit(solution)/shard_map/ppermute | solution.py:21
  66.7 40.3 %collective-permute-start.3 = (f32[8,2,128,128]{3,2,1,0:T(8,128)S(1)}, f32[8,2,128,128]{3,2,1,0:T(8,128)S(1)}, u32[]{:S(2)}, u32[]{:S(2)}) collective-permute-start(f32[8,2,128,128]{3,2,1,0:T(8,128)S(1)} %slice.181), channel_id=1, source_target_pairs={{0,4},{4,8},{8,12},{12,16},{16,20},{20,24},{24,28},{1,5},{5,9},{9,... | collective-permute-start | bytes 3145736 | tf_op jit(solution)/shard_map/ppermute | solution.py:21
  76.7 30.4 %copy-start.1 = (f32[2,256,8,128]{3,1,0,2:T(8,128)S(1)}, f32[2,256,8,128]{3,1,0,2:T(8,128)}, u32[]{:S(2)}) copy-start(f32[2,256,8,128]{3,1,0,2:T(8,128)} %copy-done) | copy-start | bytes 6291460
  107.5 27.1 %collective-permute-start.4 = (f32[8,2,128,128]{3,2,1,0:T(8,128)S(1)}, f32[8,2,128,128]{3,2,1,0:T(8,128)S(1)}, u32[]{:S(2)}, u32[]{:S(2)}) collective-permute-start(f32[8,2,128,128]{3,2,1,0:T(8,128)S(1)} %slice.182), channel_id=1, source_target_pairs={{4,0},{8,4},{12,8},{16,12},{20,16},{24,20},{28,24},{5,1},{9,5},{13... | collective-permute-start | bytes 3145736 | tf_op jit(solution)/shard_map/ppermute | solution.py:21
  135.3 127.1 %collective-permute-start.5 = (f32[2,384,128]{2,1,0:T(8,128)}, f32[2,384,128]{2,1,0:T(8,128)}, u32[]{:S(2)}, u32[]{:S(2)}) collective-permute-start(f32[2,384,128]{2,1,0:T(8,128)} %pad_maximum_fusion.1), channel_id=1, source_target_pairs={{1,0},{2,1},{3,2},{5,4},{6,5},{7,6},{9,8},{10,9},{11,10},{13,12},{... | collective-permute-start | bytes 1179656 | tf_op jit(solution)/shard_map/ppermute | solution.py:21
  137.4 289.0 %all-reduce.5.cloned.1.call-start = ((), (), s32[]{:S(2)}) async-start(), calls=%async_computation.1 | async-start | bytes 262144 | tf_op jit(solution)/shard_map/psum | solution.py:209
  262.4 1.9 copy-start.3
  264.3 0.9 copy-start.7
  265.2 0.9 copy-start.9
  271.6 9.2 %copy-start.11 = (f32[2,128,128]{2,1,0:T(8,128)}, f32[2,128,128]{2,1,0:T(8,128)S(1)}, u32[]{:S(2)}) copy-start(f32[2,128,128]{2,1,0:T(8,128)S(1)} %get-tuple-element.57) | copy-start | bytes 393220
  271.7 9.1 %collective-permute-start.6 = (f32[2,384,128]{2,1,0:T(8,128)S(1)}, f32[2,384,128]{2,1,0:T(8,128)S(1)}, u32[]{:S(2)}, u32[]{:S(2)}) collective-permute-start(f32[2,384,128]{2,1,0:T(8,128)S(1)} %slice_bitcast_fusion), channel_id=1, source_target_pairs={{0,1},{1,2},{2,3},{4,5},{5,6},{6,7},{8,9},{9,10},{10,11},{12,13},{... | collective-permute-start | bytes 1179656 | tf_op jit(solution)/shard_map/ppermute | solution.py:21
  280.8 2.0 copy-start.12
  282.8 147.6 %collective-permute-start.7 = (f32[8,2,128,128]{3,2,1,0:T(8,128)}, f32[8,2,128,128]{3,2,1,0:T(8,128)S(1)}, u32[]{:S(2)}, u32[]{:S(2)}) collective-permute-start(f32[8,2,128,128]{3,2,1,0:T(8,128)} %slice.187), channel_id=1, source_target_pairs={{0,4},{4,8},{8,12},{12,16},{16,20},{20,24},{24,28},{1,5},{5,9},{9,... | collective-permute-start | bytes 3145736 | tf_op jit(solution)/shard_map/ppermute | solution.py:21
Sparse Core Ops, SparseCore 0:
  137.6 123.2 all-reduce.2
  288.9 137.5 all-reduce.4

commit v2 on v1

v2 whole, which is shorter than its diff:
```python
import functools

import jax
import jax.numpy as jnp
import ml_dtypes
import numpy as np
from jax import lax
from jax.experimental import pallas as pl
from jax.experimental.pallas import tpu as pltpu
from jax.sharding import PartitionSpec as P

GROUP = 8
CHAIN = 4
CHUNKS = 4
ITERS = 2
STEP_OBJECT = 0.05
STEP_PROBE = 0.25
MESH = pl.DeviceIdType.MESH


def shifted(block, axis, distance):
    devices = range(lax.axis_size(axis))
    route = [(i - distance, i) for i in devices if i - distance in devices]
    return lax.ppermute(block, axis, route)


def fourier_tables(length):
    indices = np.arange(length)
    angles = (indices[:, None] * indices[None, :] % length) * (2.0 * np.pi / length)
    cos, sin = np.cos(angles), np.sin(angles)
    table = np.block([[cos, sin], [-sin, cos]])

    def parts(full):
        high = full.astype(ml_dtypes.bfloat16)
        low = (full - high.astype(np.float64)).astype(ml_dtypes.bfloat16)
        return high, low

    return (*parts(table), *parts(table.T / length))


def split(value):
    high = value.astype(jnp.bfloat16)
    low = (value - high.astype(jnp.float32)).astype(jnp.bfloat16)
    return high, low


def mm(a, b):
    return jnp.dot(a, b, preferred_element_type=jnp.float32)


def left(table_high, table_low, value):
    high, low = split(value)
    return mm(table_high, high) + mm(table_high, low) + mm(table_low, high)


def right(value, table_high, table_low):
    high, low = split(value)
    return mm(high, table_high) + mm(low, table_high) + mm(high, table_low)


def spectra(waves, wanted, on, a_hi, a_lo, t_hi, t_lo):
    count, side = len(waves), waves[0].shape[0]
    spans = [slice(m * side, (m + 1) * side) for m in range(count)]
    half = right(jnp.concatenate(waves, axis=0), t_hi[...], t_lo[...])
    half = jnp.concatenate(
        [
            jnp.concatenate([half[span, :side] for span in spans], axis=1),
            jnp.concatenate([half[span, side:] for span in spans], axis=1),
        ],
        axis=0,
    )
    far = left(a_hi[...], a_lo[...], half)
    far_re, far_im = far[:side], far[side:]
    power = far_re * far_re + far_im * far_im
    scale = jnp.concatenate(
        [jnp.full((1, side), jnp.where(live, 2.0, 0.0), jnp.float32) for live in on], axis=1
    )
    weight = scale * (power - jnp.concatenate(wanted, axis=1))
    half = left(
        t_hi[...], t_lo[...], jnp.concatenate([weight * far_re, weight * far_im], axis=0)
    )
    half = jnp.concatenate(
        [jnp.concatenate([half[:side, span], half[side:, span]], axis=1) for span in spans],
        axis=0,
    )
    near = right(half, a_hi[...], a_lo[...])
    return [near[span] for span in spans]


def slots_kernel(
    live_ref, pos_ref, own, below, beside, corner, prb, a_hi, a_lo, t_hi, t_lo, measured,
    own_out, down_out, right_out, corner_out, pgrad_out,
    ext, grad, pgrad, values, sems,
):
    _, rows, width = own.shape
    side = prb.shape[1]
    strips = width // side
    top, low = pl.ds(0, rows), pl.ds(rows, side)
    copies = [pltpu.make_async_copy(measured, values, sems.at[0])]
    for strip in range(strips):
        columns = pl.ds(strip * side, side)
        copies.append(
            pltpu.make_async_copy(own.at[:, :, columns], ext.at[strip, :, top, :], sems.at[2 * strip + 1])
        )
        copies.append(
            pltpu.make_async_copy(below.at[:, :, columns], ext.at[strip, :, low, :], sems.at[2 * strip + 2])
        )
    copies.append(
        pltpu.make_async_copy(beside, ext.at[strips, :, top, :], sems.at[2 * strips + 1])
    )
    copies.append(
        pltpu.make_async_copy(corner, ext.at[strips, :, low, :], sems.at[2 * strips + 2])
    )
    for copy in copies:
        copy.start()
    for strip in range(strips + 1):
        grad[strip] = jnp.zeros(grad.shape[1:], jnp.float32)
    pgrad[...] = jnp.zeros_like(pgrad)
    for copy in copies:
        copy.wait()

    live = live_ref[0]
    lane = lax.broadcasted_iota(jnp.int32, (side, side), 1)

    def block(index, _):
        places = []
        objects = []
        waves = []
        for member in range(GROUP):
            slot = index * GROUP + member
            on = slot < live
            row = jnp.where(on, pos_ref[2 * slot], 0)
            col = jnp.where(on, pos_ref[2 * slot + 1], 0)
            strip = col // side
            shift = col - strip * side
            keep = lane >= shift
            back = (side - shift) % side
            window = pl.ds(row, side)

            def take(part):
                here = ext[strip, part, window, :]
                there = ext[strip + 1, part, window, :]
                return pltpu.roll(jnp.where(keep, here, there), back, 1)

            obj_re, obj_im = take(0), take(1)
            psi_re = prb[0] * obj_re - prb[1] * obj_im
            psi_im = prb[0] * obj_im + prb[1] * obj_re
            places.append((slot, on, strip, shift, window, keep))
            objects.append((obj_re, obj_im))
            waves.append(jnp.concatenate([psi_re, psi_im], axis=1))
        near = []
        for first in range(0, GROUP, CHAIN):
            members = slice(first, first + CHAIN)
            near += spectra(waves[members], [values[p[0]] for p in places[members]],
                            [p[1] for p in places[members]], a_hi, a_lo, t_hi, t_lo)
        sum_re = jnp.zeros((side, side), jnp.float32)
        sum_im = jnp.zeros((side, side), jnp.float32)
        for member in range(GROUP):
            slot, on, strip, shift, window, keep = places[member]
            obj_re, obj_im = objects[member]
            back_re, back_im = near[member][:, :side], near[member][:, side:]
            sum_re += obj_re * back_re + obj_im * back_im
            sum_im += obj_re * back_im - obj_im * back_re
            for part, value in (
                (0, prb[0] * back_re + prb[1] * back_im),
                (1, prb[0] * back_im - prb[1] * back_re),
            ):
                turned = pltpu.roll(value, shift, 1)
                grad[strip, part, window, :] += jnp.where(keep, turned, 0.0)
                grad[strip + 1, part, window, :] += jnp.where(keep, 0.0, turned)
        pgrad[0] += sum_re
        pgrad[1] += sum_im
        return 0

    lax.fori_loop(0, (live + GROUP - 1) // GROUP, block, 0)

    pieces, deep, _ = pgrad_out.shape
    per = 2 * side // pieces
    for piece in range(pieces):
        part, start = divmod(piece * per, side)
        pgrad_out[piece, :per] = pgrad[part, start : start + per]
        pgrad_out[piece, per:] = jnp.full((deep - per, side), live.astype(jnp.float32))
    copies = []
    for strip in range(strips):
        ext[strip, :, :rows] -= STEP_OBJECT * grad[strip, :, :rows]
        columns = pl.ds(strip * side, side)
        copies.append(
            pltpu.make_async_copy(grad.at[strip, :, low, :], down_out.at[:, :, columns], sems.at[2 * strip])
        )
        copies.append(
            pltpu.make_async_copy(ext.at[strip, :, top, :], own_out.at[:, :, columns], sems.at[2 * strip + 1])
        )
        copies[-2].start()
        copies[-1].start()
    copies.append(
        pltpu.make_async_copy(grad.at[strips, :, top, :], right_out, sems.at[2 * strips])
    )
    copies.append(
        pltpu.make_async_copy(grad.at[strips, :, low, :], corner_out, sems.at[2 * strips + 1])
    )
    copies[-2].start()
    copies[-1].start()
    for copy in copies:
        copy.wait()


def slots_call(live, places, own, below, beside, corner, probe, tables, measured, pieces):
    _, rows, width = own.shape
    side = probe.shape[1]
    strips = width // side
    shape = (strips + 1, 2, rows + side, side)
    smem = pl.BlockSpec(memory_space=pltpu.SMEM)
    vmem = pl.BlockSpec(memory_space=pltpu.VMEM)
    hbm = pl.BlockSpec(memory_space=pl.ANY)
    sent = (pieces, 2 * side // pieces + 8, side)
    return pl.pallas_call(
        slots_kernel,
        out_shape=[
            jax.ShapeDtypeStruct(of, jnp.float32)
            for of in (own.shape, below.shape, beside.shape, corner.shape, sent)
        ],
        in_specs=[smem, smem, hbm, hbm, hbm, hbm, vmem, vmem, vmem, vmem, vmem, hbm],
        out_specs=[hbm, hbm, hbm, hbm, vmem],
        scratch_shapes=[
            pltpu.VMEM(shape, jnp.float32),
            pltpu.VMEM(shape, jnp.float32),
            pltpu.VMEM(probe.shape, jnp.float32),
            pltpu.VMEM(measured.shape, jnp.float32),
            pltpu.SemaphoreType.DMA((2 * strips + 3,)),
        ],
        compiler_params=pltpu.CompilerParams(vmem_limit_bytes=40 * 1024 * 1024),
    )(live, places, own, below, beside, corner, probe, *tables, measured)


class Mover:
    def __init__(self, sends, recvs):
        self.sends, self.recvs, self.used = sends, recvs, 0

    def make(self, src, dst, peer):
        index, self.used = self.used, self.used + 1
        return pltpu.make_async_remote_copy(
            src_ref=src, dst_ref=dst, send_sem=self.sends.at[index], recv_sem=self.recvs.at[index],
            device_id=peer, device_id_type=MESH,
        )


def exchange_kernel(n_row, n_col, spill, halo, *refs):
    refs = list(refs)
    own = refs.pop(0)
    if spill:
        down, right_rim, far, sent, prb = refs[:5]
        del refs[:5]
    if halo:
        below, beside, corner = refs[:3]
        del refs[:3]
    if spill:
        now, out = refs[:2]
        del refs[:2]
        got_down, got_right, got_far, from_rows, from_cols = refs[:5]
        del refs[:5]
    else:
        now = own
    mover = Mover(*refs)
    _, rows, width = now.shape
    row, col = lax.axis_index("row"), lax.axis_index("col")
    row_peers = [lax.rem(row + d, n_row) for d in range(1, n_row)]
    col_peers = [lax.rem(col + d, n_col) for d in range(1, n_col)]
    next_row, last_row = row_peers[0], row_peers[-1]
    next_col, last_col = col_peers[0], col_peers[-1]
    has_prev_row, has_next_row = row > 0, row < n_row - 1
    has_prev_col, has_next_col = col > 0, col < n_col - 1
    has_prev_far = jnp.logical_and(has_prev_row, has_prev_col)
    has_next_far = jnp.logical_and(has_next_row, has_next_col)

    barrier = pltpu.get_barrier_semaphore()
    greeted = [(peer, col) for peer in row_peers] + [(row, peer) for peer in col_peers]
    greeted += [(next_row, next_col), (last_row, last_col)]
    for peer in greeted:
        pl.semaphore_signal(barrier, inc=1, device_id=peer, device_id_type=MESH)
    pl.semaphore_wait(barrier, len(greeted))

    edge = corner.shape[1] if halo else far.shape[1]
    step = width // CHUNKS
    spans = [pl.ds(c * step, step) for c in range(CHUNKS)]
    ends = []

    def begin(copy, here):
        if here is None:
            copy.start()
        else:
            pl.when(here)(copy.start)
        ends.append((copy.wait_send, here))

    def finish(wait, here):
        if here is None:
            wait()
        else:
            pl.when(here)(wait)

    if spill:
        first = [
            mover.make(sent.at[peer], from_rows.at[d], (peer, col))
            for d, peer in enumerate(row_peers)
        ]
        for copy in first:
            begin(copy, None)
        downs = [
            mover.make(down.at[:, :, span], got_down.at[:, :, span], (next_row, col))
            for span in spans
        ]
        rights = mover.make(right_rim, got_right, (row, next_col))
        fars = mover.make(far, got_far, (next_row, next_col))
        begin(fars, has_next_far)
        begin(rights, has_next_col)
        for copy in downs:
            begin(copy, has_next_row)
        now[...] = own[...]
        for copy in first:
            copy.wait_recv()
        total = sent[row]
        for d in range(n_row - 1):
            total += from_rows[d]
        from_cols[col] = total
        second = [
            mover.make(from_cols.at[col], from_cols.at[col], (row, peer)) for peer in col_peers
        ]
        for copy in second:
            begin(copy, None)
        finish(rights.wait_recv, has_prev_col)
        finish(fars.wait_recv, has_prev_far)

        @pl.when(has_prev_col)
        def _():
            now[:, :, :edge] -= STEP_OBJECT * got_right[...]

        @pl.when(has_prev_far)
        def _():
            now[:, :edge, :edge] -= STEP_OBJECT * got_far[...]

        for copy in second:
            copy.wait_recv()
        total = from_cols[0]
        for d in range(1, n_col):
            total += from_cols[d]
        per = prb.shape[1]
        out[row] = prb[row] - STEP_PROBE * total[:per] / total[per : per + 1]
        third = [mover.make(out.at[row], out.at[row], (peer, col)) for peer in row_peers]
        for copy in third:
            begin(copy, None)

    if halo:
        ups = [
            mover.make(now.at[:, pl.ds(0, edge), span], below.at[:, :, span], (last_row, col))
            for span in spans
        ]
        lefts = mover.make(now.at[:, :, pl.ds(0, edge)], beside, (row, last_col))
        backs = mover.make(
            now.at[:, pl.ds(0, edge), pl.ds(0, edge)], corner, (last_row, last_col)
        )
    for c in range(CHUNKS):
        if spill:
            finish(downs[c].wait_recv, has_prev_row)

            @pl.when(has_prev_row)
            def _():
                cells = slice(c * step, (c + 1) * step)
                now[:, :edge, cells] -= STEP_OBJECT * got_down[:, :, cells]

        if halo:
            if c == 0:
                begin(backs, has_prev_far)
                begin(lefts, has_prev_col)
            begin(ups[c], has_prev_row)
    if halo:
        finish(backs.wait_recv, has_next_far)
        finish(lefts.wait_recv, has_next_col)
        for copy in ups:
            finish(copy.wait_recv, has_next_row)
    if spill:
        for copy in third:
            copy.wait_recv()
    for wait, here in ends:
        finish(wait, here)


def exchange_call(number, spill, halo, n_row, n_col, edge, own, *rest):
    _, rows, width = own.shape
    vmem = pl.BlockSpec(memory_space=pltpu.VMEM)
    hbm = pl.BlockSpec(memory_space=pl.ANY)
    args, shapes, specs, scratch, count = [own, *rest], [], [], [], 0
    if halo:
        shapes += [(2, edge, width), (2, rows, edge), (2, edge, edge)]
        specs += [hbm] * 3
        count += CHUNKS + 2
    if spill:
        sent, probe = rest[3:]
        args[-1] = probe.reshape(n_row, -1, edge)
        shapes += [own.shape, args[-1].shape]
        specs += [vmem] * 2
        count += CHUNKS + 2 + 2 * (n_row - 1) + n_col - 1
        scratch = [
            (2, edge, width), (2, rows, edge), (2, edge, edge),
            (n_row - 1, *sent.shape[1:]), (n_col, *sent.shape[1:]),
        ]
    results = list(pl.pallas_call(
        functools.partial(exchange_kernel, n_row, n_col, spill, halo),
        out_shape=[jax.ShapeDtypeStruct(shape, jnp.float32) for shape in shapes],
        in_specs=[vmem, hbm, hbm, hbm, vmem, vmem] if spill else [hbm],
        out_specs=specs,
        scratch_shapes=[pltpu.VMEM(shape, jnp.float32) for shape in scratch]
        + [pltpu.SemaphoreType.DMA((count,))] * 2,
        compiler_params=pltpu.CompilerParams(
            collective_id=number, has_side_effects=True, vmem_limit_bytes=24 * 1024 * 1024
        ),
    )(*args))
    if spill:
        results[-1] = results[-1].reshape(probe.shape)
    return results


def body(object_field, probe, position, live_count, intensity):
    side = probe.shape[1]
    n_row, n_col = lax.axis_size("row"), lax.axis_size("col")
    tables = [jnp.asarray(t) for t in fourier_tables(side)]
    places = position[0, 0].reshape(-1)
    measured = intensity[0, 0]
    live = live_count.reshape(1)
    now = object_field
    halos = exchange_call(0, False, True, n_row, n_col, side, now)
    for sweep in range(ITERS):
        parts = slots_call(live, places, now, *halos, probe, tables, measured, n_row)
        more = sweep < ITERS - 1
        *halos, now, probe = exchange_call(
            2 - int(more), True, more, n_row, n_col, side, *parts, probe
        )
    return (now, probe)


def solution(mesh):
    placed = (
        P(None, "row", "col"),
        P(),
        P("row", "col", None, None),
        P("row", "col"),
        P("row", "col", None, None, None),
    )
    return jax.shard_map(
        body, mesh=mesh, in_specs=placed, out_specs=(P(None, "row", "col"), P()), check_vma=False
    )
```

time: 447 us -> 183 us (0.41)
  waiting for transfers between devices: 298 us -> 0 us
  Pallas kernels: 11.6 us -> 168 us
  starting transfers between devices: 45.7 us -> 0 us
  blocking collectives: 42.6 us -> 0 us
  between operations: 15 us -> 1.44 us
  local copies, waits for them, and re-layouts: 22.3 us -> 10.9 us
  other arithmetic: 8.72 us -> 0 us
    psum x2 -> x0, waiting for transfers between devices: 218 us -> none  [body(): probe_total = lax.psum(probe_grad, ('row', 'col'))]
    pallas_call x2 -> x5, Pallas kernels: 11.6 us -> 168 us  [the longest x3 157 us: exchange_call(): pl.pallas_call(functools.partial(exchange_kernel, n_row, n_col, spill, ha...]
    ppermute x8 -> x0, waiting for transfers between devices: 79.6 us -> none  [shifted(): return lax.ppermute(block, axis, route)]
    ppermute x8 -> x0, starting transfers between devices: 45.6 us -> none  [shifted(): return lax.ppermute(block, axis, route)]
    psum x1 -> x0, blocking collectives: 42.6 us -> none  [body(): live_total = lax.psum(live.astype(jnp.float32), ('row', 'col'))]
  transfers between devices with their start and end apart: 10 -> 0, of which waited for: 8 -> 0; matrix products, arithmetic and copies ran while one was open for 2% -> 0% of each run, Pallas kernels for 0% -> 0%
where the time goes in v2:
time: 183 us; the launch traced here: 181 us
  Pallas kernels  168 us (92%)
  local copies, waits for them, and re-layouts  10.9 us (6%)
    pallas_call x3, Pallas kernels, exchange_call(): pl.pallas_call(functools.partial(exchange_kernel, n_row, n_col, spill, ha...  157 us
    pallas_call x2, Pallas kernels, slots_call(): pl.pallas_call(slots_kernel, out_shape=[jax.ShapeDtypeStruct(of, jnp.floa...  11.4 us
    unnamed x31, local copies, waits for them, and re-layouts  10.8 us

profile of v2, /device:TPU:20, one launch (start us, length us, event | category | flops | bytes accessed | tf_op | source)
XLA Modules:
  0.0 180.8 jit_solution(7413733508068085138)
XLA Ops:
  1.3 0.8 copy.12
  2.0 0.1 reshape_squeeze.3.pos_ref
  2.2 0.0 copy-start.2
  2.2 1.6 copy-done.2
  3.8 0.0 copy-start.3
  3.8 29.3 %shard_map.104 = (f32[2,128,1024]{2,1,0:T(8,128)S(1)}, f32[2,256,128]{2,1,0:T(8,128)S(1)}, f32[2,128,128]{2,1,0:T(8,128)S(1)}) custom-call(f32[2,256,1024]{2,1,0:T(8,128)S(1)} %copy-done.2), custom_call_target="tpu_custom_call" | custom-call | tf_op jit(solution)/shard_map/pallas_call | solution.py:405
  33.1 0.0 copy-done.3
  33.1 0.0 copy-start
  33.1 1.9 %copy-done = f32[1,1,48,128,128]{4,3,2,1,0:T(8,128)S(1)} copy-done((f32[1,1,48,128,128]{4,3,2,1,0:T(8,128)S(1)}, f32[1,1,48,128,128]{4,3,2,1,0:T(8,128)}, u32[]{:S(2)}) %copy-start) | copy-done | bytes 3145752
  35.0 0.0 copy-start.4
  35.0 0.9 copy-done.4
  35.9 0.0 copy-start.6
  35.9 0.9 copy-done.6
  36.8 0.0 copy-start.8
  36.8 0.9 copy-done.8
  37.7 0.0 copy-start.10
  37.7 0.9 copy-done.10
  38.6 0.0 copy-start.12
  38.6 0.9 copy-done.12
  39.5 0.0 copy-start.13
  39.5 5.7 %shard_map.105 = (f32[2,256,1024]{2,1,0:T(8,128)S(1)}, f32[2,128,1024]{2,1,0:T(8,128)S(1)}, f32[2,256,128]{2,1,0:T(8,128)S(1)}, f32[2,128,128]{2,1,0:T(8,128)S(1)}, f32[8,40,128]{2,1,0:T(8,128)S(1)}) custom-call(s32[1]{0:T(128)} %bitcast.7.live_ref, s32[96]{0:T(128)S(1)} %reshape_squeeze.3.pos_ref, f32[2,256,1024]{2,1,0:T(8,128)S(1)} %copy-done.3, ...), custom_call_target="tpu_custom_call" | custom-call | tf_op jit(solution)/shard_map/pallas_call | solution.py:216
  45.2 0.0 copy-start.1
  45.3 0.0 copy-start.5
  45.3 0.0 copy-start.7
  45.3 0.0 copy-start.9
  45.3 0.0 copy-start.11
  45.3 0.0 copy-done.13
  45.3 78.8 %shard_map.106 = (f32[2,128,1024]{2,1,0:T(8,128)S(1)}, f32[2,256,128]{2,1,0:T(8,128)S(1)}, f32[2,128,128]{2,1,0:T(8,128)S(1)}, f32[2,256,1024]{2,1,0:T(8,128)S(1)}, f32[8,32,128]{2,1,0:T(8,128)S(1)}) custom-call(f32[2,256,1024]{2,1,0:T(8,128)S(1)} %get-tuple-element.25.refs_0_, f32[2,128,1024]{2,1,0:T(8,128)S(1)} %get-tuple-element.26.refs_1_, ...), custom_call_target="tpu_custom_call" | custom-call | tf_op jit(solution)/shard_map/pallas_call | solution.py:405
  124.2 0.0 copy-done.1
  124.2 0.0 copy-done.5
  124.2 0.0 copy-done.7
  124.2 0.0 copy-done.9
  124.2 0.0 copy-done.11
  124.2 5.7 %shard_map.107 = (f32[2,256,1024]{2,1,0:T(8,128)S(1)}, f32[2,128,1024]{2,1,0:T(8,128)S(1)}, f32[2,256,128]{2,1,0:T(8,128)S(1)}, f32[2,128,128]{2,1,0:T(8,128)S(1)}, f32[8,40,128]{2,1,0:T(8,128)S(1)}) custom-call(s32[1]{0:T(128)} %bitcast.8.live_ref, s32[96]{0:T(128)S(1)} %reshape_squeeze.3.pos_ref, f32[2,256,1024]{2,1,0:T(8,128)S(1)} %get-tuple-element.30.own, ...), custom_call_target="tpu_custom_call" | custom-call | tf_op jit(solution)/shard_map/pallas_call | solution.py:216
  129.9 48.9 %shard_map.108 = (f32[2,256,1024]{2,1,0:T(8,128)S(1)}, f32[8,32,128]{2,1,0:T(8,128)S(1)}) custom-call(f32[2,256,1024]{2,1,0:T(8,128)S(1)} %get-tuple-element.35.refs_0_, f32[2,128,1024]{2,1,0:T(8,128)S(1)} %get-tuple-element.36.refs_1_, f32[2,256,128]{2,1,0:T(8,128)S(1)} %get-tuple-element.37.refs_2_, f32[2,128,128]{2,1,0:T(8,128)S(1)} %get-tuple-element.38.refs_3_, ...), custom_call_target="tpu_custom_call" | custom-call | tf_op jit(solution)/shard_map/pallas_call | solution.py:405
  178.8 1.3 copy.16
  180.1 0.7 copy.17
Async XLA Ops:
  2.2 1.6 copy-start.2
  3.8 29.4 %copy-start.3 = (f32[2,256,1024]{2,1,0:T(8,128)S(1)}, f32[2,256,1024]{2,1,0:T(8,128)}, u32[]{:S(2)}) copy-start(f32[2,256,1024]{2,1,0:T(8,128)} %own.1) | copy-start | bytes 6291460
  33.1 1.9 %copy-start = (f32[1,1,48,128,128]{4,3,2,1,0:T(8,128)S(1)}, f32[1,1,48,128,128]{4,3,2,1,0:T(8,128)}, u32[]{:S(2)}) copy-start(f32[1,1,48,128,128]{4,3,2,1,0:T(8,128)} %param.13) | copy-start | bytes 9437188
  35.0 0.9 copy-start.4
  35.9 0.9 copy-start.6
  36.8 0.9 copy-start.8
  37.7 0.9 copy-start.10
  38.6 0.9 copy-start.12
  39.5 5.8 %copy-start.13 = (f32[2,128,128]{2,1,0:T(8,128)S(1)}, f32[2,128,128]{2,1,0:T(8,128)}, u32[]{:S(2)}) copy-start(f32[2,128,128]{2,1,0:T(8,128)} %prb.1) | copy-start | bytes 393220
  45.2 78.9 %copy-start.1 = (f32[1,1,48,128,128]{4,3,2,1,0:T(8,128)S(1)}, f32[1,1,48,128,128]{4,3,2,1,0:T(8,128)}, u32[]{:S(2)}) copy-start(f32[1,1,48,128,128]{4,3,2,1,0:T(8,128)} %param.13) | copy-start | bytes 9437188
  45.3 78.9 %copy-start.5 = (bf16[256,256]{1,0:T(8,128)(2,1)S(1)}, bf16[256,256]{1,0:T(8,128)(2,1)}, u32[]{:S(2)}) copy-start(bf16[256,256]{1,0:T(8,128)(2,1)} %constant.11.clone.t_lo) | copy-start | bytes 393220
  45.3 78.9 %copy-start.7 = (bf16[256,256]{1,0:T(8,128)(2,1)S(1)}, bf16[256,256]{1,0:T(8,128)(2,1)}, u32[]{:S(2)}) copy-start(bf16[256,256]{1,0:T(8,128)(2,1)} %constant.10.clone.t_hi) | copy-start | bytes 393220
  45.3 78.9 %copy-start.9 = (bf16[256,256]{1,0:T(8,128)(2,1)S(1)}, bf16[256,256]{1,0:T(8,128)(2,1)}, u32[]{:S(2)}) copy-start(bf16[256,256]{1,0:T(8,128)(2,1)} %constant.9.clone.a_lo) | copy-start | bytes 393220
  45.3 78.9 %copy-start.11 = (bf16[256,256]{1,0:T(8,128)(2,1)S(1)}, bf16[256,256]{1,0:T(8,128)(2,1)}, u32[]{:S(2)}) copy-start(bf16[256,256]{1,0:T(8,128)(2,1)} %constant.8.clone.a_hi) | copy-start | bytes 393220

commit v3 on v2

--- a/solution.py
+++ b/solution.py
@@ -9,7 +9,7 @@
 from jax.experimental.pallas import tpu as pltpu
 from jax.sharding import PartitionSpec as P
 
-GROUP = 8
+GROUP = 16
 CHAIN = 4
 CHUNKS = 4
 ITERS = 2
@@ -88,15 +88,20 @@
 
 
 def slots_kernel(
-    live_ref, pos_ref, own, below, beside, corner, prb, a_hi, a_lo, t_hi, t_lo, measured,
+    live_ref, pos_ref, own, below, beside, corner, prb_in, tables_in, measured,
     own_out, down_out, right_out, corner_out, pgrad_out,
-    ext, grad, pgrad, values, sems,
+    ext, grad, pgrad, values, prb, tables, sems,
 ):
     _, rows, width = own.shape
     side = prb.shape[1]
     strips = width // side
     top, low = pl.ds(0, rows), pl.ds(rows, side)
-    copies = [pltpu.make_async_copy(measured, values, sems.at[0])]
+    copies = [
+        pltpu.make_async_copy(measured, values, sems.at[0]),
+        pltpu.make_async_copy(prb_in, prb, sems.at[2 * strips + 3]),
+        pltpu.make_async_copy(tables_in, tables, sems.at[2 * strips + 4]),
+    ]
+    a_hi, a_lo, t_hi, t_lo = (tables.at[i] for i in range(4))
     for strip in range(strips):
         columns = pl.ds(strip * side, side)
         copies.append(
@@ -212,6 +217,7 @@
     smem = pl.BlockSpec(memory_space=pltpu.SMEM)
     vmem = pl.BlockSpec(memory_space=pltpu.VMEM)
     hbm = pl.BlockSpec(memory_space=pl.ANY)
+    pinned = pl.BlockSpec(memory_space=pltpu.HBM)
     sent = (pieces, 2 * side // pieces + 8, side)
     return pl.pallas_call(
         slots_kernel,
@@ -219,17 +225,19 @@
             jax.ShapeDtypeStruct(of, jnp.float32)
             for of in (own.shape, below.shape, beside.shape, corner.shape, sent)
         ],
-        in_specs=[smem, smem, hbm, hbm, hbm, hbm, vmem, vmem, vmem, vmem, vmem, hbm],
+        in_specs=[smem, smem, hbm, hbm, hbm, hbm, hbm, pinned, pinned],
         out_specs=[hbm, hbm, hbm, hbm, vmem],
         scratch_shapes=[
             pltpu.VMEM(shape, jnp.float32),
             pltpu.VMEM(shape, jnp.float32),
             pltpu.VMEM(probe.shape, jnp.float32),
             pltpu.VMEM(measured.shape, jnp.float32),
-            pltpu.SemaphoreType.DMA((2 * strips + 3,)),
+            pltpu.VMEM(probe.shape, jnp.float32),
+            pltpu.VMEM(tables.shape, tables.dtype),
+            pltpu.SemaphoreType.DMA((2 * strips + 5,)),
         ],
         compiler_params=pltpu.CompilerParams(vmem_limit_bytes=40 * 1024 * 1024),
-    )(live, places, own, below, beside, corner, probe, *tables, measured)
+    )(live, places, own, below, beside, corner, probe, tables, measured)
 
 
 class Mover:
@@ -256,8 +264,8 @@
     if spill:
         now, out = refs[:2]
         del refs[:2]
-        got_down, got_right, got_far, from_rows, from_cols = refs[:5]
-        del refs[:5]
+        got_down, got_right, got_far, from_rows, from_cols, head = refs[:6]
+        del refs[:6]
     else:
         now = own
     mover = Mover(*refs)
@@ -269,12 +277,11 @@
     next_col, last_col = col_peers[0], col_peers[-1]
     has_prev_row, has_next_row = row > 0, row < n_row - 1
     has_prev_col, has_next_col = col > 0, col < n_col - 1
-    has_prev_far = jnp.logical_and(has_prev_row, has_prev_col)
-    has_next_far = jnp.logical_and(has_next_row, has_next_col)
+    passes_corner = jnp.logical_and(has_next_row, has_prev_col)
+    takes_corner = jnp.logical_and(has_next_row, has_next_col)
 
     barrier = pltpu.get_barrier_semaphore()
     greeted = [(peer, col) for peer in row_peers] + [(row, peer) for peer in col_peers]
-    greeted += [(next_row, next_col), (last_row, last_col)]
     for peer in greeted:
         pl.semaphore_signal(barrier, inc=1, device_id=peer, device_id_type=MESH)
     pl.semaphore_wait(barrier, len(greeted))
@@ -282,6 +289,7 @@
     edge = corner.shape[1] if halo else far.shape[1]
     step = width // CHUNKS
     spans = [pl.ds(c * step, step) for c in range(CHUNKS)]
+    order = [1, 0, *range(2, CHUNKS)] if spill else list(range(CHUNKS))
     ends = []
 
     def begin(copy, here):
@@ -304,16 +312,25 @@
         ]
         for copy in first:
             begin(copy, None)
+        rights = mover.make(right_rim, got_right, (row, next_col))
+        fars = mover.make(far, got_far, (row, next_col))
+        begin(fars, has_next_col)
+        begin(rights, has_next_col)
         downs = [
-            mover.make(down.at[:, :, span], got_down.at[:, :, span], (next_row, col))
-            for span in spans
+            mover.make(
+                down.at[:, :, span] if c else head, got_down.at[:, :, span], (next_row, col)
+            )
+            for c, span in enumerate(spans)
         ]
-        rights = mover.make(right_rim, got_right, (row, next_col))
-        fars = mover.make(far, got_far, (next_row, next_col))
-        begin(fars, has_next_far)
-        begin(rights, has_next_col)
-        for copy in downs:
-            begin(copy, has_next_row)
+        begin(downs[1], has_next_row)
+        head[...] = down[:, :, :step]
+        finish(fars.wait_recv, has_prev_col)
+
+        @pl.when(has_prev_col)
+        def _():
+            head[:, :, :edge] += got_far[...]
+
+        begin(downs[0], has_next_row)
         now[...] = own[...]
         for copy in first:
             copy.wait_recv()
@@ -326,27 +343,12 @@
         ]
         for copy in second:
             begin(copy, None)
+        begin(downs[2], has_next_row)
         finish(rights.wait_recv, has_prev_col)
-        finish(fars.wait_recv, has_prev_far)
 
         @pl.when(has_prev_col)
         def _():
             now[:, :, :edge] -= STEP_OBJECT * got_right[...]
-
-        @pl.when(has_prev_far)
-        def _():
-            now[:, :edge, :edge] -= STEP_OBJECT * got_far[...]
-
-        for copy in second:
-            copy.wait_recv()
-        total = from_cols[0]
-        for d in range(1, n_col):
-            total += from_cols[d]
-        per = prb.shape[1]
-        out[row] = prb[row] - STEP_PROBE * total[:per] / total[per : per + 1]
-        third = [mover.make(out.at[row], out.at[row], (peer, col)) for peer in row_peers]
-        for copy in third:
-            begin(copy, None)
 
     if halo:
         ups = [
@@ -354,10 +356,8 @@
             for span in spans
         ]
         lefts = mover.make(now.at[:, :, pl.ds(0, edge)], beside, (row, last_col))
-        backs = mover.make(
-            now.at[:, pl.ds(0, edge), pl.ds(0, edge)], corner, (last_row, last_col)
-        )
-    for c in range(CHUNKS):
+        passed = mover.make(below.at[:, :, pl.ds(0, edge)], corner, (row, last_col))
+    for c in order:
         if spill:
             finish(downs[c].wait_recv, has_prev_row)
 
@@ -368,14 +368,28 @@
 
         if halo:
             if c == 0:
-                begin(backs, has_prev_far)
                 begin(lefts, has_prev_col)
             begin(ups[c], has_prev_row)
+        if spill and c == order[0]:
+            for copy in second:
+                copy.wait_recv()
+            total = from_cols[0]
+            for d in range(1, n_col):
+                total += from_cols[d]
+            per = prb.shape[1]
+            out[row] = prb[row] - STEP_PROBE * total[:per] / total[per : per + 1]
+            third = [mover.make(out.at[row], out.at[row], (peer, col)) for peer in row_peers]
+            for copy in third:
+                begin(copy, None)
+            for copy in downs[3:]:
+                begin(copy, has_next_row)
     if halo:
-        finish(backs.wait_recv, has_next_far)
+        finish(ups[0].wait_recv, has_next_row)
+        begin(passed, passes_corner)
         finish(lefts.wait_recv, has_next_col)
-        for copy in ups:
+        for copy in ups[1:]:
             finish(copy.wait_recv, has_next_row)
+        finish(passed.wait_recv, takes_corner)
     if spill:
         for copy in third:
             copy.wait_recv()
@@ -387,6 +401,7 @@
     _, rows, width = own.shape
     vmem = pl.BlockSpec(memory_space=pltpu.VMEM)
     hbm = pl.BlockSpec(memory_space=pl.ANY)
+    pinned = pl.BlockSpec(memory_space=pltpu.HBM)
     args, shapes, specs, scratch, count = [own, *rest], [], [], [], 0
     if halo:
         shapes += [(2, edge, width), (2, rows, edge), (2, edge, edge)]
@@ -400,18 +415,20 @@
         count += CHUNKS + 2 + 2 * (n_row - 1) + n_col - 1
         scratch = [
             (2, edge, width), (2, rows, edge), (2, edge, edge),
-            (n_row - 1, *sent.shape[1:]), (n_col, *sent.shape[1:]),
+            (n_row - 1, *sent.shape[1:]), (n_col, *sent.shape[1:]), (2, edge, width // CHUNKS),
         ]
     results = list(pl.pallas_call(
         functools.partial(exchange_kernel, n_row, n_col, spill, halo),
         out_shape=[jax.ShapeDtypeStruct(shape, jnp.float32) for shape in shapes],
-        in_specs=[vmem, hbm, hbm, hbm, vmem, vmem] if spill else [hbm],
+        in_specs=[vmem, vmem, hbm, hbm, vmem, vmem] if spill else [pinned],
         out_specs=specs,
         scratch_shapes=[pltpu.VMEM(shape, jnp.float32) for shape in scratch]
         + [pltpu.SemaphoreType.DMA((count,))] * 2,
         compiler_params=pltpu.CompilerParams(
-            collective_id=number, has_side_effects=True, vmem_limit_bytes=24 * 1024 * 1024
+            collective_id=number, has_side_effects=True,
+            vmem_limit_bytes=(24 if spill else 4) * 1024 * 1024,
         ),
+        cost_estimate=pl.CostEstimate(flops=0, transcendentals=0, bytes_accessed=100 * 1024 * 1024),
     )(*args))
     if spill:
         results[-1] = results[-1].reshape(probe.shape)
@@ -421,7 +438,7 @@
 def body(object_field, probe, position, live_count, intensity):
     side = probe.shape[1]
     n_row, n_col = lax.axis_size("row"), lax.axis_size("col")
-    tables = [jnp.asarray(t) for t in fourier_tables(side)]
+    tables = jnp.asarray(np.stack(fourier_tables(side)))
     places = position[0, 0].reshape(-1)
     measured = intensity[0, 0]
     live = live_count.reshape(1)

time: 183 us -> 167 us (0.913); the launches traced: 181 us -> 168 us
  Pallas kernels: 168 us -> 158 us
  local copies, waits for them, and re-layouts: 10.9 us -> 8.3 us
    pallas_call x3, Pallas kernels: 157 us -> 141 us  [exchange_call(): pl.pallas_call(functools.partial(exchange_kernel, n_row, n_col, spill, ha...]
    pallas_call x2, Pallas kernels: 11.4 us -> 16.7 us  [slots_call(): pl.pallas_call(slots_kernel, out_shape=[jax.ShapeDtypeStruct(of, jnp.floa...]
    unnamed x31 -> x19, local copies, waits for them, and re-layouts: 10.8 us -> 8.18 us
where the time goes in v3:
time: 167 us; the launch traced here: 168 us
  Pallas kernels  158 us (95%)
  local copies, waits for them, and re-layouts  8.3 us (5%)
    pallas_call x3, Pallas kernels, exchange_call(): pl.pallas_call(functools.partial(exchange_kernel, n_row, n_col, spill, ha...  141 us
    pallas_call x2, Pallas kernels, slots_call(): pl.pallas_call(slots_kernel, out_shape=[jax.ShapeDtypeStruct(of, jnp.floa...  16.7 us
    unnamed x19, local copies, waits for them, and re-layouts  8.18 us

profile of v3, /device:TPU:20, one launch (start us, length us, event | category | flops | bytes accessed | tf_op | source)
XLA Modules:
  0.0 167.9 jit_solution(460931078654281369)
XLA Ops:
  1.3 0.8 copy.9
  2.0 0.1 reshape_squeeze.3.pos_ref
  2.2 0.0 copy-start.2
  2.2 1.6 copy-done.2
  3.8 0.0 copy-start.3
  3.8 26.1 %shard_map.77 = (f32[2,128,1024]{2,1,0:T(8,128)S(1)}, f32[2,256,128]{2,1,0:T(8,128)S(1)}, f32[2,128,128]{2,1,0:T(8,128)S(1)}) custom-call(f32[2,256,1024]{2,1,0:T(8,128)S(1)} %copy-done.2), custom_call_target="tpu_custom_call" | custom-call | bytes 104857600 | tf_op jit(solution)/shard_map/pallas_call | solution.py:420
  29.8 0.0 copy-done.3
  29.8 0.0 copy-start
  29.9 1.9 %copy-done = f32[1,1,48,128,128]{4,3,2,1,0:T(8,128)S(1)} copy-done((f32[1,1,48,128,128]{4,3,2,1,0:T(8,128)S(1)}, f32[1,1,48,128,128]{4,3,2,1,0:T(8,128)}, u32[]{:S(2)}) %copy-start) | copy-done | bytes 3145752
  31.7 0.0 copy-start.4
  31.7 1.0 copy-done.4
  32.8 0.0 copy-start.6
  32.8 0.9 copy-done.6
  33.7 0.0 copy-start.7
  33.7 8.3 %shard_map.78 = (f32[2,256,1024]{2,1,0:T(8,128)S(1)}, f32[2,128,1024]{2,1,0:T(8,128)S(1)}, f32[2,256,128]{2,1,0:T(8,128)S(1)}, f32[2,128,128]{2,1,0:T(8,128)S(1)}, f32[8,40,128]{2,1,0:T(8,128)S(1)}) custom-call(s32[1]{0:T(128)} %bitcast.7.live_ref, s32[96]{0:T(128)S(1)} %reshape_squeeze.3.pos_ref, f32[2,256,1024]{2,1,0:T(8,128)S(1)} %copy-done.3, ...), custom_call_target="tpu_custom_call" | custom-call | tf_op jit(solution)/shard_map/pallas_call | solution.py:222
  41.9 0.0 copy-start.1
  42.0 0.0 copy-start.5
  42.0 0.0 copy-done.7
  42.0 71.4 %shard_map.79 = (f32[2,128,1024]{2,1,0:T(8,128)S(1)}, f32[2,256,128]{2,1,0:T(8,128)S(1)}, f32[2,128,128]{2,1,0:T(8,128)S(1)}, f32[2,256,1024]{2,1,0:T(8,128)S(1)}, f32[8,32,128]{2,1,0:T(8,128)S(1)}) custom-call(f32[2,256,1024]{2,1,0:T(8,128)S(1)} %get-tuple-element.25.refs_0_, f32[2,128,1024]{2,1,0:T(8,128)S(1)} %get-tuple-element.26.refs_1_, ...), custom_call_target="tpu_custom_call" | custom-call | bytes 104857600 | tf_op jit(solution)/shard_map/pallas_call | solution.py:420
  113.4 0.0 copy-done.1
  113.4 0.0 copy-done.5
  113.4 8.4 %shard_map.80 = (f32[2,256,1024]{2,1,0:T(8,128)S(1)}, f32[2,128,1024]{2,1,0:T(8,128)S(1)}, f32[2,256,128]{2,1,0:T(8,128)S(1)}, f32[2,128,128]{2,1,0:T(8,128)S(1)}, f32[8,40,128]{2,1,0:T(8,128)S(1)}) custom-call(s32[1]{0:T(128)} %bitcast.8.live_ref, s32[96]{0:T(128)S(1)} %reshape_squeeze.3.pos_ref, f32[2,256,1024]{2,1,0:T(8,128)S(1)} %get-tuple-element.30.own, ...), custom_call_target="tpu_custom_call" | custom-call | tf_op jit(solution)/shard_map/pallas_call | solution.py:222
  121.9 44.0 %shard_map.81 = (f32[2,256,1024]{2,1,0:T(8,128)S(1)}, f32[8,32,128]{2,1,0:T(8,128)S(1)}) custom-call(f32[2,256,1024]{2,1,0:T(8,128)S(1)} %get-tuple-element.35.refs_0_, f32[2,128,1024]{2,1,0:T(8,128)S(1)} %get-tuple-element.36.refs_1_, f32[2,256,128]{2,1,0:T(8,128)S(1)} %get-tuple-element.37.refs_2_, f32[2,128,128]{2,1,0:T(8,128)S(1)} %get-tuple-element.38.refs_3_, ...), custom_call_target="tpu_custom_call" | custom-call | bytes 104857600 | tf_op jit(solution)/shard_map/pallas_call | solution.py:420
  165.9 1.3 copy.13
  167.2 0.7 copy.14
Async XLA Ops:
  2.2 1.6 copy-start.2
  3.8 26.1 %copy-start.3 = (f32[2,256,1024]{2,1,0:T(8,128)S(1)}, f32[2,256,1024]{2,1,0:T(8,128)}, u32[]{:S(2)}) copy-start(f32[2,256,1024]{2,1,0:T(8,128)} %own.1) | copy-start | bytes 6291460
  29.8 1.9 %copy-start = (f32[1,1,48,128,128]{4,3,2,1,0:T(8,128)S(1)}, f32[1,1,48,128,128]{4,3,2,1,0:T(8,128)}, u32[]{:S(2)}) copy-start(f32[1,1,48,128,128]{4,3,2,1,0:T(8,128)} %param.10) | copy-start | bytes 9437188
  31.7 1.0 copy-start.4
  32.8 0.9 copy-start.6
  33.7 8.3 %copy-start.7 = (f32[2,128,128]{2,1,0:T(8,128)S(1)}, f32[2,128,128]{2,1,0:T(8,128)}, u32[]{:S(2)}) copy-start(f32[2,128,128]{2,1,0:T(8,128)} %prb_in.1) | copy-start | bytes 393220
  41.9 71.5 %copy-start.1 = (f32[1,1,48,128,128]{4,3,2,1,0:T(8,128)S(1)}, f32[1,1,48,128,128]{4,3,2,1,0:T(8,128)}, u32[]{:S(2)}) copy-start(f32[1,1,48,128,128]{4,3,2,1,0:T(8,128)} %param.10) | copy-start | bytes 9437188
  42.0 71.5 %copy-start.5 = (bf16[4,256,256]{2,1,0:T(8,128)(2,1)S(1)}, bf16[4,256,256]{2,1,0:T(8,128)(2,1)}, u32[]{:S(2)}) copy-start(bf16[4,256,256]{2,1,0:T(8,128)(2,1)} %constant.2.clone.tables_in) | copy-start | bytes 1572868

commit v4 on v3

--- a/solution.py
+++ b/solution.py
@@ -50,12 +50,18 @@
 
 def left(table_high, table_low, value):
     high, low = split(value)
-    return mm(table_high, high) + mm(table_high, low) + mm(table_low, high)
+    return mm(
+        jnp.concatenate([table_high, table_low, table_high], axis=1),
+        jnp.concatenate([high, high, low], axis=0),
+    )
 
 
 def right(value, table_high, table_low):
     high, low = split(value)
-    return mm(high, table_high) + mm(low, table_high) + mm(high, table_low)
+    return mm(
+        jnp.concatenate([high, low, high], axis=1),
+        jnp.concatenate([table_high, table_high, table_low], axis=0),
+    )
 
 
 def spectra(waves, wanted, on, a_hi, a_lo, t_hi, t_lo):
@@ -426,7 +432,7 @@
         + [pltpu.SemaphoreType.DMA((count,))] * 2,
         compiler_params=pltpu.CompilerParams(
             collective_id=number, has_side_effects=True,
-            vmem_limit_bytes=(24 if spill else 4) * 1024 * 1024,
+            vmem_limit_bytes=(24 if spill else 60) * 1024 * 1024,
         ),
         cost_estimate=pl.CostEstimate(flops=0, transcendentals=0, bytes_accessed=100 * 1024 * 1024),
     )(*args))

time: 167 us -> 168 us (level)
  Pallas kernels: 158 us -> 156 us
    pallas_call x3, Pallas kernels: 141 us -> 139 us  [exchange_call(): pl.pallas_call(functools.partial(exchange_kernel, n_row, n_col, spill, ha...]
    unnamed x19 -> x23, local copies, waits for them, and re-layouts: 8.18 us -> 9.67 us
where the time goes in v4:
time: 168 us; the launch traced here: 167 us
  Pallas kernels  156 us (93%)
  local copies, waits for them, and re-layouts  9.79 us (6%)
    pallas_call x3, Pallas kernels, exchange_call(): pl.pallas_call(functools.partial(exchange_kernel, n_row, n_col, spill, ha...  139 us
    pallas_call x2, Pallas kernels, slots_call(): pl.pallas_call(slots_kernel, out_shape=[jax.ShapeDtypeStruct(of, jnp.floa...  17 us
    unnamed x23, local copies, waits for them, and re-layouts  9.67 us

profile of v4, /device:TPU:20, one launch (start us, length us, event | category | flops | bytes accessed | tf_op | source)
XLA Modules:
  0.0 167.4 jit_solution(13397895124461629668)
XLA Ops:
  0.6 0.0 copy-start.2
  1.4 0.8 copy.9
  2.2 0.1 reshape_squeeze.3.pos_ref
  2.3 26.5 %shard_map.77 = (f32[2,128,1024]{2,1,0:T(8,128)}, f32[2,256,128]{2,1,0:T(8,128)}, f32[2,128,128]{2,1,0:T(8,128)}) custom-call(f32[2,256,1024]{2,1,0:T(8,128)} %own.1), custom_call_target="tpu_custom_call" | custom-call | bytes 104857600 | tf_op jit(solution)/shard_map/pallas_call | solution.py:426
  28.8 0.0 copy-done.2
  28.8 0.0 copy-start
  28.8 1.9 %copy-done = f32[1,1,48,128,128]{4,3,2,1,0:T(8,128)S(1)} copy-done((f32[1,1,48,128,128]{4,3,2,1,0:T(8,128)S(1)}, f32[1,1,48,128,128]{4,3,2,1,0:T(8,128)}, u32[]{:S(2)}) %copy-start) | copy-done | bytes 3145752
  30.7 0.0 copy-start.3
  30.7 1.0 copy-done.3
  31.7 0.0 copy-start.5
  31.7 1.2 copy-done.5
  33.0 0.0 copy-start.6
  33.0 0.9 copy-done.6
  33.9 0.0 copy-start.8
  33.9 0.9 copy-done.8
  34.8 0.0 copy-start.9
  34.8 0.9 copy-done.9
  35.7 0.0 copy-start.7
  35.7 8.4 %shard_map.78 = (f32[2,256,1024]{2,1,0:T(8,128)S(1)}, f32[2,128,1024]{2,1,0:T(8,128)S(1)}, f32[2,256,128]{2,1,0:T(8,128)S(1)}, f32[2,128,128]{2,1,0:T(8,128)S(1)}, f32[8,40,128]{2,1,0:T(8,128)S(1)}) custom-call(s32[1]{0:T(128)} %bitcast.7.live_ref, s32[96]{0:T(128)S(1)} %reshape_squeeze.3.pos_ref, f32[2,256,1024]{2,1,0:T(8,128)S(1)} %copy-done.2, ...), custom_call_target="tpu_custom_call" | custom-call | tf_op jit(solution)/shard_map/pallas_call | solution.py:228
  44.1 0.0 copy-start.1
  44.1 0.0 copy-start.4
  44.1 0.0 copy-done.7
  44.2 69.8 %shard_map.79 = (f32[2,128,1024]{2,1,0:T(8,128)S(1)}, f32[2,256,128]{2,1,0:T(8,128)S(1)}, f32[2,128,128]{2,1,0:T(8,128)S(1)}, f32[2,256,1024]{2,1,0:T(8,128)S(1)}, f32[8,32,128]{2,1,0:T(8,128)S(1)}) custom-call(f32[2,256,1024]{2,1,0:T(8,128)S(1)} %get-tuple-element.25.refs_0_, f32[2,128,1024]{2,1,0:T(8,128)S(1)} %get-tuple-element.26.refs_1_, ...), custom_call_target="tpu_custom_call" | custom-call | bytes 104857600 | tf_op jit(solution)/shard_map/pallas_call | solution.py:426
  113.9 0.0 copy-done.1
  113.9 0.0 copy-done.4
  113.9 8.6 %shard_map.80 = (f32[2,256,1024]{2,1,0:T(8,128)S(1)}, f32[2,128,1024]{2,1,0:T(8,128)S(1)}, f32[2,256,128]{2,1,0:T(8,128)S(1)}, f32[2,128,128]{2,1,0:T(8,128)S(1)}, f32[8,40,128]{2,1,0:T(8,128)S(1)}) custom-call(s32[1]{0:T(128)} %bitcast.8.live_ref, s32[96]{0:T(128)S(1)} %reshape_squeeze.3.pos_ref, f32[2,256,1024]{2,1,0:T(8,128)S(1)} %get-tuple-element.30.own, ...), custom_call_target="tpu_custom_call" | custom-call | tf_op jit(solution)/shard_map/pallas_call | solution.py:228
  122.5 42.9 %shard_map.81 = (f32[2,256,1024]{2,1,0:T(8,128)S(1)}, f32[8,32,128]{2,1,0:T(8,128)S(1)}) custom-call(f32[2,256,1024]{2,1,0:T(8,128)S(1)} %get-tuple-element.35.refs_0_, f32[2,128,1024]{2,1,0:T(8,128)S(1)} %get-tuple-element.36.refs_1_, f32[2,256,128]{2,1,0:T(8,128)S(1)} %get-tuple-element.37.refs_2_, f32[2,128,128]{2,1,0:T(8,128)S(1)} %get-tuple-element.38.refs_3_, ...), custom_call_target="tpu_custom_call" | custom-call | bytes 104857600 | tf_op jit(solution)/shard_map/pallas_call | solution.py:426
  165.4 1.3 copy.13
  166.7 0.7 copy.14
Async XLA Ops:
  0.6 28.2 %copy-start.2 = (f32[2,256,1024]{2,1,0:T(8,128)S(1)}, f32[2,256,1024]{2,1,0:T(8,128)}, u32[]{:S(2)}) copy-start(f32[2,256,1024]{2,1,0:T(8,128)} %own.1) | copy-start | bytes 6291460
  28.8 1.9 %copy-start = (f32[1,1,48,128,128]{4,3,2,1,0:T(8,128)S(1)}, f32[1,1,48,128,128]{4,3,2,1,0:T(8,128)}, u32[]{:S(2)}) copy-start(f32[1,1,48,128,128]{4,3,2,1,0:T(8,128)} %param.10) | copy-start | bytes 9437188
  30.7 1.0 copy-start.3
  31.7 1.2 copy-start.5
  33.0 0.9 copy-start.6
  33.9 0.9 copy-start.8
  34.8 0.9 copy-start.9
  35.7 8.4 %copy-start.7 = (f32[2,128,128]{2,1,0:T(8,128)S(1)}, f32[2,128,128]{2,1,0:T(8,128)}, u32[]{:S(2)}) copy-start(f32[2,128,128]{2,1,0:T(8,128)} %prb_in.1) | copy-start | bytes 393220
  44.1 69.8 %copy-start.1 = (f32[1,1,48,128,128]{4,3,2,1,0:T(8,128)S(1)}, f32[1,1,48,128,128]{4,3,2,1,0:T(8,128)}, u32[]{:S(2)}) copy-start(f32[1,1,48,128,128]{4,3,2,1,0:T(8,128)} %param.10) | copy-start | bytes 9437188
  44.1 69.8 %copy-start.4 = (bf16[4,256,256]{2,1,0:T(8,128)(2,1)S(1)}, bf16[4,256,256]{2,1,0:T(8,128)(2,1)}, u32[]{:S(2)}) copy-start(bf16[4,256,256]{2,1,0:T(8,128)(2,1)} %constant.2.clone.tables_in) | copy-start | bytes 1572868

commit v5 on v4

--- a/solution.py
+++ b/solution.py
@@ -242,7 +242,7 @@
             pltpu.VMEM(tables.shape, tables.dtype),
             pltpu.SemaphoreType.DMA((2 * strips + 5,)),
         ],
-        compiler_params=pltpu.CompilerParams(vmem_limit_bytes=40 * 1024 * 1024),
+        compiler_params=pltpu.CompilerParams(vmem_limit_bytes=60 * 1024 * 1024),
     )(live, places, own, below, beside, corner, probe, tables, measured)
 
 
@@ -270,8 +270,9 @@
     if spill:
         now, out = refs[:2]
         del refs[:2]
-        got_down, got_right, got_far, from_rows, from_cols, head = refs[:6]
-        del refs[:6]
+        got_down, got_right, got_far, from_rows, from_cols, head, mine, prb_mine = refs[:8]
+        local = refs.pop()
+        del refs[:8]
     else:
         now = own
     mover = Mover(*refs)
@@ -286,6 +287,17 @@
     passes_corner = jnp.logical_and(has_next_row, has_prev_col)
     takes_corner = jnp.logical_and(has_next_row, has_next_col)
 
+    if spill:
+        step = now.shape[2] // CHUNKS
+        fetches = [
+            pltpu.make_async_copy(down.at[:, :, pl.ds(0, step)], head, local.at[0]),
+            pltpu.make_async_copy(sent.at[row], mine, local.at[1]),
+            pltpu.make_async_copy(prb.at[row], prb_mine, local.at[2]),
+            pltpu.make_async_copy(own, now, local.at[3]),
+        ]
+        for copy in fetches:
+            copy.start()
+
     barrier = pltpu.get_barrier_semaphore()
     greeted = [(peer, col) for peer in row_peers] + [(row, peer) for peer in col_peers]
     for peer in greeted:
@@ -329,7 +341,8 @@
             for c, span in enumerate(spans)
         ]
         begin(downs[1], has_next_row)
-        head[...] = down[:, :, :step]
+        for copy in fetches:
+            copy.wait()
         finish(fars.wait_recv, has_prev_col)
 
         @pl.when(has_prev_col)
@@ -337,10 +350,9 @@
             head[:, :, :edge] += got_far[...]
 
         begin(downs[0], has_next_row)
-        now[...] = own[...]
         for copy in first:
             copy.wait_recv()
-        total = sent[row]
+        total = mine[...]
         for d in range(n_row - 1):
             total += from_rows[d]
         from_cols[col] = total
@@ -383,7 +395,7 @@
             for d in range(1, n_col):
                 total += from_cols[d]
             per = prb.shape[1]
-            out[row] = prb[row] - STEP_PROBE * total[:per] / total[per : per + 1]
+            out[row] = prb_mine[...] - STEP_PROBE * total[:per] / total[per : per + 1]
             third = [mover.make(out.at[row], out.at[row], (peer, col)) for peer in row_peers]
             for copy in third:
                 begin(copy, None)
@@ -407,7 +419,6 @@
     _, rows, width = own.shape
     vmem = pl.BlockSpec(memory_space=pltpu.VMEM)
     hbm = pl.BlockSpec(memory_space=pl.ANY)
-    pinned = pl.BlockSpec(memory_space=pltpu.HBM)
     args, shapes, specs, scratch, count = [own, *rest], [], [], [], 0
     if halo:
         shapes += [(2, edge, width), (2, rows, edge), (2, edge, edge)]
@@ -422,17 +433,19 @@
         scratch = [
             (2, edge, width), (2, rows, edge), (2, edge, edge),
             (n_row - 1, *sent.shape[1:]), (n_col, *sent.shape[1:]), (2, edge, width // CHUNKS),
+            sent.shape[1:], args[-1].shape[1:],
         ]
     results = list(pl.pallas_call(
         functools.partial(exchange_kernel, n_row, n_col, spill, halo),
         out_shape=[jax.ShapeDtypeStruct(shape, jnp.float32) for shape in shapes],
-        in_specs=[vmem, vmem, hbm, hbm, vmem, vmem] if spill else [pinned],
+        in_specs=[hbm] * len(args),
         out_specs=specs,
         scratch_shapes=[pltpu.VMEM(shape, jnp.float32) for shape in scratch]
-        + [pltpu.SemaphoreType.DMA((count,))] * 2,
+        + [pltpu.SemaphoreType.DMA((count,))] * 2
+        + [pltpu.SemaphoreType.DMA((4,))] * int(spill),
         compiler_params=pltpu.CompilerParams(
             collective_id=number, has_side_effects=True,
-            vmem_limit_bytes=(24 if spill else 60) * 1024 * 1024,
+            vmem_limit_bytes=60 * 1024 * 1024,
         ),
         cost_estimate=pl.CostEstimate(flops=0, transcendentals=0, bytes_accessed=100 * 1024 * 1024),
     )(*args))

time: 168 us -> 174 us (1.036)
  Pallas kernels: 156 us -> 166 us
  local copies, waits for them, and re-layouts: 9.79 us -> 5.32 us
    pallas_call x2, Pallas kernels: 17 us -> 23.6 us  [slots_call(): pl.pallas_call(slots_kernel, out_shape=[jax.ShapeDtypeStruct(of, jnp.floa...]
    unnamed x23 -> x5, local copies, waits for them, and re-layouts: 9.67 us -> 4.62 us
    pallas_call x3, Pallas kernels: 139 us -> 142 us  [exchange_call(): pl.pallas_call(functools.partial(exchange_kernel, n_row, n_col, spill, ha...]
where the time goes in v5:
time: 174 us; the launch traced here: 173 us
  Pallas kernels  166 us (95%)
  local copies, waits for them, and re-layouts  5.32 us (3%)
    pallas_call x3, Pallas kernels, exchange_call(): pl.pallas_call(functools.partial(exchange_kernel, n_row, n_col, spill, ha...  142 us
    pallas_call x2, Pallas kernels, slots_call(): pl.pallas_call(slots_kernel, out_shape=[jax.ShapeDtypeStruct(of, jnp.floa...  23.6 us
    unnamed x5, local copies, waits for them, and re-layouts  4.62 us

profile of v5, /device:TPU:20, one launch (start us, length us, event | category | flops | bytes accessed | tf_op | source)
XLA Modules:
  0.0 172.6 jit_solution(2323774807668838706)
XLA Ops:
  1.3 0.8 copy.9
  2.0 0.7 reshape_squeeze.3.pos_ref
  2.7 26.4 %shard_map.77 = (f32[2,128,1024]{2,1,0:T(8,128)}, f32[2,256,128]{2,1,0:T(8,128)}, f32[2,128,128]{2,1,0:T(8,128)}) custom-call(f32[2,256,1024]{2,1,0:T(8,128)} %own.1), custom_call_target="tpu_custom_call" | custom-call | bytes 104857600 | tf_op jit(solution)/shard_map/pallas_call | solution.py:438
  29.1 11.8 %shard_map.78 = (f32[2,256,1024]{2,1,0:T(8,128)}, f32[2,128,1024]{2,1,0:T(8,128)}, f32[2,256,128]{2,1,0:T(8,128)}, f32[2,128,128]{2,1,0:T(8,128)}, f32[8,40,128]{2,1,0:T(8,128)}) custom-call(s32[1]{0:T(128)} %bitcast.7.live_ref, s32[96]{0:T(128)} %reshape_squeeze.3.pos_ref, f32[2,256,1024]{2,1,0:T(8,128)} %own.1, f32[2,128,1024]{2,1,0:T(8,128)} %get-tuple-element.22.below, ...), custom_call_target="tpu_custom_call" | custom-call | tf_op jit(solution)/shard_map/pallas_call | solution.py:228
  41.0 71.0 %shard_map.79 = (f32[2,128,1024]{2,1,0:T(8,128)}, f32[2,256,128]{2,1,0:T(8,128)}, f32[2,128,128]{2,1,0:T(8,128)}, f32[2,256,1024]{2,1,0:T(8,128)}, f32[8,32,128]{2,1,0:T(8,128)}) custom-call(f32[2,256,1024]{2,1,0:T(8,128)} %get-tuple-element.25.refs_0_, f32[2,128,1024]{2,1,0:T(8,128)} %get-tuple-element.26.refs_1_, ...), custom_call_target="tpu_custom_call" | custom-call | bytes 104857600 | tf_op jit(solution)/shard_map/pallas_call | solution.py:438
  111.9 11.8 %shard_map.80 = (f32[2,256,1024]{2,1,0:T(8,128)}, f32[2,128,1024]{2,1,0:T(8,128)}, f32[2,256,128]{2,1,0:T(8,128)}, f32[2,128,128]{2,1,0:T(8,128)}, f32[8,40,128]{2,1,0:T(8,128)}) custom-call(s32[1]{0:T(128)} %bitcast.8.live_ref, s32[96]{0:T(128)} %reshape_squeeze.3.pos_ref, f32[2,256,1024]{2,1,0:T(8,128)} %get-tuple-element.30.own, ...), custom_call_target="tpu_custom_call" | custom-call | tf_op jit(solution)/shard_map/pallas_call | solution.py:228
  123.7 45.0 %shard_map.81 = (f32[2,256,1024]{2,1,0:T(8,128)}, f32[8,32,128]{2,1,0:T(8,128)}) custom-call(f32[2,256,1024]{2,1,0:T(8,128)} %get-tuple-element.35.refs_0_, f32[2,128,1024]{2,1,0:T(8,128)} %get-tuple-element.36.refs_1_, f32[2,256,128]{2,1,0:T(8,128)} %get-tuple-element.37.refs_2_, f32[2,128,128]{2,1,0:T(8,128)} %get-tuple-element.38.refs_3_, ...), custom_call_target="tpu_custom_call" | custom-call | bytes 104857600 | tf_op jit(solution)/shard_map/pallas_call | solution.py:438
  168.7 0.0 copy-start
  168.7 3.2 %copy.13 = f32[2,256,1024]{2,1,0:T(8,128)} copy(f32[2,256,1024]{2,1,0:T(8,128)} %get-tuple-element.44) | data formatting | bytes 4194304
  171.9 0.0 copy-done
  171.9 0.7 copy.14
Async XLA Ops:
  168.7 3.2 %copy-start = (f32[8,32,128]{2,1,0:T(8,128)S(1)}, f32[8,32,128]{2,1,0:T(8,128)}, u32[]{:S(2)}) copy-start(f32[8,32,128]{2,1,0:T(8,128)} %get-tuple-element.41) | copy-start | bytes 393220
